TPU v7x, 128 devices: a whole 4x4x4 slice. The times are simulated.
128 devices in a mesh: section: 16 (over y, z), tensor: 8 (over x, core).
Axes of the slice: x: 4, y: 4, z: 4, core: 2. Of those that a mesh axis runs over, the one named last changes fastest.
Arguments:
- hidden: bfloat16 [512, 8192], P('section', 'tensor'), may hold values from -16 to 16
- ref_hidden: bfloat16 [512, 8192], P('section', 'tensor'), may hold values from -16 to 16
- w_policy: bfloat16 [65536, 8192], P(('section', 'tensor')), may hold values from -0.5 to 0.5
- w_ref: bfloat16 [65536, 8192], P(('section', 'tensor')), may hold values from -0.5 to 0.5
- token_ids: int32 [512], replicated, may hold values from 0 to 65535
- loss_mask: int32 [512], replicated, may hold values 0 or 1
- advantages: float32 [512], replicated, may hold values from -4 to 4
Outputs:
- grad_hidden: float32 [512, 8192], P('section', 'tensor')
- grad_head: bfloat16 [65536, 8192], P(('section', 'tensor'))
All inputs are finite; a program needn't handle non-finite values.
Results may differ from a plain program's by a relative error of at most 0.005.
Values may be sent and summed in bfloat16 or wider, within the bound.
A program may use at most 128 MiB of HBM per device.

v0:
```python
import jax
import jax.numpy as jnp
from jax import lax
from jax.sharding import PartitionSpec as P

loss_scale = 4.0
penalty_weight = 0.2


def shards(hidden, ref_hidden, w_policy, w_ref, token_ids, loss_mask, advantages):
    features, ref_features = (
        lax.all_gather(hidden, "tensor", axis=1, tiled=True),
        lax.all_gather(ref_hidden, "tensor", axis=1, tiled=True),
    )
    full_hidden = lax.all_gather(features, "section", axis=0, tiled=True)
    ref_logits = jnp.einsum(
        "td,vd->tv",
        lax.all_gather(ref_features, "section", axis=0, tiled=True),
        w_ref,
        preferred_element_type=jnp.float32,
    )
    logits = jnp.einsum("td,vd->tv", full_hidden, w_policy, preferred_element_type=jnp.float32)
    vocab_width = w_policy.shape[0]
    offset = (
        lax.axis_index("section") * lax.axis_size("tensor") + lax.axis_index("tensor")
    ) * vocab_width
    maximum, ref_maximum = lax.pmax(
        (jnp.max(logits, axis=1), jnp.max(ref_logits, axis=1)), ("section", "tensor")
    )
    mass, ref_mass = lax.psum(
        (
            jnp.sum(jnp.exp(logits - maximum[:, None]), axis=1),
            jnp.sum(jnp.exp(ref_logits - ref_maximum[:, None]), axis=1),
        ),
        ("section", "tensor"),
    )
    log_norm = maximum + jnp.log(mass)
    ref_norm = ref_maximum + jnp.log(ref_mass)
    log_probs = logits - log_norm[:, None]
    ref_log_probs = ref_logits - ref_norm[:, None]
    probabilities = jnp.exp(log_probs)
    divergence = lax.psum(
        jnp.sum(probabilities * (log_probs - ref_log_probs), axis=1), ("section", "tensor")
    )
    column = offset + lax.broadcasted_iota(jnp.int32, logits.shape, 1)
    target = (column == token_ids[:, None]).astype(jnp.float32)
    weight = loss_scale * loss_mask.astype(jnp.float32)[:, None]
    grad_logits = (
        weight
        * (
            advantages[:, None] * (probabilities - target)
            + penalty_weight * probabilities * (log_probs - ref_log_probs - divergence[:, None])
        )
    ).astype(jnp.bfloat16)
    grad_head = jnp.einsum(
        "tv,td->vd", grad_logits, full_hidden, preferred_element_type=jnp.float32
    ).astype(jnp.bfloat16)
    row_terms = lax.psum_scatter(
        jnp.dot(grad_logits, w_policy, preferred_element_type=jnp.float32),
        "section",
        scatter_dimension=0,
        tiled=True,
    )
    grad_hidden = lax.psum_scatter(row_terms, "tensor", scatter_dimension=1, tiled=True)
    return (grad_hidden, grad_head)


def solution(mesh):
    placed = (
        P("section", "tensor"),
        P("section", "tensor"),
        P(("section", "tensor"), None),
        P(("section", "tensor"), None),
        P(),
        P(),
        P(),
    )
    return jax.shard_map(
        shards,
        mesh=mesh,
        in_specs=placed,
        out_specs=(P("section", "tensor"), P(("section", "tensor"), None)),
        check_vma=False,
    )
```

profile of v0, /device:TPU:0, one launch (start us, length us, event | category | flops | bytes accessed | tf_op | source)
XLA Modules:
  0.0 529.8 jit_solution(9150419596771400122)
XLA Ops:
  7.2 0.0 all-gather.5.cloned.1.call-start
  7.2 14.9 %all_gather.14 = bf16[32,8192]{1,0:T(8,128)(2,1)} all-gather(bf16[32,1024]{1,0:T(8,128)(2,1)} %param.8), channel_id=1, replica_groups=mesh['section'=16,'tensor'=8] {'tensor'}, dimensions={1}, use_global_device_ids=true | all-gather | bytes 589824 | tf_op jit(solution)/shard_map/all_gather | solution.py:13
  22.1 0.0 all-gather.5.cloned.1.call-update
  22.1 0.0 all-gather.3.cloned.1.call-start
  22.1 14.4 %all_gather.12 = bf16[32,8192]{1,0:T(8,128)(2,1)} all-gather(bf16[32,1024]{1,0:T(8,128)(2,1)} %param.7), channel_id=1, replica_groups=mesh['section'=16,'tensor'=8] {'tensor'}, dimensions={1}, use_global_device_ids=true | all-gather | bytes 589824 | tf_op jit(solution)/shard_map/all_gather | solution.py:12
  36.6 0.0 all-gather.3.cloned.1.call-update
  36.6 0.0 reduce-scatter.3.cloned.1.call-start
  36.7 0.7 convert_multiply_fusion
  37.4 57.6 %all-gather.5.cloned.1.call-done = bf16[512,8192]{1,0:T(8,128)(2,1)} async-done(((bf16[32,8192]{1,0:T(8,128)(2,1)}), bf16[512,8192]{1,0:T(8,128)(2,1)}) %all-gather.5.cloned.1.call-update) | async-done | bytes 8388624 | tf_op jit(solution)/shard_map/all_gather | solution.py:18
  94.9 9.5 %fusion = (f32[512]{0:T(512)S(1)}, f32[512,512]{0,1:T(8,128)S(1)}) fusion(bf16[512,8192]{1,0:T(8,128)(2,1)} %all-gather.5.cloned.1.call-done, bf16[512,8192]{1,0:T(8,128)(2,1)} %param.10), kind=kOutput, calls=%fused_computation.10 | convolution fusion | flops 4295228928 | bytes 17827840 | tf_op jit(solution)/shard_map/td,vd->tv/dot_general | solution.py:16
  104.4 0.0 copy-start
  104.4 0.0 copy-start.1
  104.4 63.1 %all-gather.3.cloned.1.call-done = bf16[512,8192]{1,0:T(8,128)(2,1)} async-done(((bf16[32,8192]{1,0:T(8,128)(2,1)}), bf16[512,8192]{1,0:T(8,128)(2,1)}) %all-gather.3.cloned.1.call-update) | async-done | bytes 8388624 | tf_op jit(solution)/shard_map/all_gather | solution.py:15
  167.5 9.4 %fusion.1 = (f32[512]{0:T(512)S(1)}, f32[512,512]{0,1:T(8,128)S(1)}) fusion(bf16[512,8192]{1,0:T(8,128)(2,1)} %all-gather.3.cloned.1.call-done, bf16[512,8192]{1,0:T(8,128)(2,1)} %param.9), kind=kOutput, calls=%fused_computation.11 | convolution fusion | flops 4295228928 | bytes 17827840 | tf_op jit(solution)/shard_map/td,vd->tv/dot_general | solution.py:22
  177.0 64.5 %all-reduce.1 = (f32[512]{0:T(512)S(1)}, f32[512]{0:T(512)S(1)}) all-reduce(f32[512]{0:T(512)S(1)} %get-tuple-element.6, f32[512]{0:T(512)S(1)} %get-tuple-element.8), channel_id=1, replica_groups=mesh['section'=16,'tensor'=8] {'section','tensor'}, use_global_device_ids=true, to_apply=%region_5.0 | all-reduce | flops 1024 | bytes 8192 | tf_op jit(solution)/shard_map/pmax | solution.py:27
  241.5 0.3 exponential_reduce_fusion
  241.8 64.3 %all-reduce = (f32[512]{0:T(512)S(1)}, f32[512]{0:T(512)S(1)}) all-reduce(f32[512]{0:T(512)S(1)} %get-tuple-element.10, f32[512]{0:T(512)S(1)} %get-tuple-element.11), channel_id=1, replica_groups=mesh['section'=16,'tensor'=8] {'section','tensor'}, use_global_device_ids=true, to_apply=%region_7.0 | all-reduce | flops 1024 | bytes 8192 | tf_op jit(solution)/shard_map/psum | solution.py:30
  306.1 0.3 multiply_reduce_fusion
  306.4 62.4 %psum.23 = f32[512]{0:T(512)S(1)} all-reduce(f32[512]{0:T(512)S(1)} %multiply_reduce_fusion), channel_id=1, replica_groups=mesh['section'=16,'tensor'=8] {'section','tensor'}, use_global_device_ids=true, to_apply=%region_9.0 | all-reduce | flops 512 | bytes 4096 | tf_op jit(solution)/shard_map/psum | solution.py:42
  368.9 0.0 copy-done
  368.9 0.0 copy-done.1
  368.9 0.5 multiply_convert_fusion
  369.4 11.5 %fusion.2 = f32[512,8192]{1,0:T(8,128)} fusion(bf16[512,512]{0,1:T(8,128)(2,1)S(1)} %multiply_convert_fusion, bf16[512,8192]{1,0:T(8,128)(2,1)} %param.9), kind=kOutput, calls=%fused_computation.12 | convolution fusion | flops 4294967296 | bytes 25690112 | tf_op jit(solution)/shard_map/dot_general | solution.py:59
  380.9 0.0 reduce-scatter.3.cloned.1.call-update
  380.9 0.0 reduce-scatter.5.cloned.1.call-start
  381.0 108.2 %reduce-scatter.3.cloned.1.call-done = f32[32,8192]{1,0:T(8,128)} async-done(((f32[512,8192]{1,0:T(8,128)}), f32[32,8192]{1,0:T(8,128)}) %reduce-scatter.3.cloned.1.call-update) | async-done | bytes 1048592 | tf_op jit(solution)/shard_map/reduce_scatter | solution.py:58
  489.2 0.0 reduce-scatter.5.cloned.1.call-update
  489.2 10.3 %convolution_convert_fusion = bf16[512,8192]{1,0:T(8,128)(2,1)} fusion(bf16[512,512]{0,1:T(8,128)(2,1)S(1)} %multiply_convert_fusion, bf16[512,8192]{1,0:T(8,128)(2,1)} %all-gather.3.cloned.1.call-done), kind=kOutput, calls=%fused_computation | convolution fusion | flops 4299161600 | bytes 17301504 | tf_op jit(solution)/shard_map/tv,td->vd/dot_general | solution.py:55
  499.6 23.7 %reduce-scatter.5.cloned.1.call-done = f32[32,1024]{1,0:T(8,128)} async-done(((f32[32,8192]{1,0:T(8,128)}), f32[32,1024]{1,0:T(8,128)}) %reduce-scatter.5.cloned.1.call-update) | async-done | bytes 131088 | tf_op jit(solution)/shard_map/reduce_scatter | solution.py:64
  (3 shorter events, 0.0 us)
Async XLA Ops:
  7.2 87.7 %all-gather.5.cloned.1.call-start = ((), (), s32[]{:S(2)}) async-start(), calls=%async_computation.3 | async-start | bytes 8912896 | tf_op jit(solution)/shard_map/all_gather | solution.py:18
  22.1 145.4 %all-gather.3.cloned.1.call-start = ((), (), s32[]{:S(2)}) async-start(), calls=%async_computation.2 | async-start | bytes 8912896 | tf_op jit(solution)/shard_map/all_gather | solution.py:15
  36.6 452.6 %reduce-scatter.3.cloned.1.call-start = ((), (), s32[]{:S(2)}) async-start(), calls=%async_computation.4 | async-start | bytes 17825792 | tf_op jit(solution)/shard_map/reduce_scatter | solution.py:58
  104.4 264.5 %copy-start = (s32[512]{0:T(512)S(1)}, s32[512]{0:T(512)}, u32[]{:S(2)}) copy-start(s32[512]{0:T(512)} %param.11) | copy-start | bytes 6148
  104.4 264.5 %copy-start.1 = (f32[512]{0:T(512)S(1)}, f32[512]{0:T(512)}, u32[]{:S(2)}) copy-start(f32[512]{0:T(512)} %param.13) | copy-start | bytes 6148
  380.9 142.3 %reduce-scatter.5.cloned.1.call-start = ((), (), s32[]{:S(2)}) async-start(), calls=%async_computation.5 | async-start | bytes 1179648 | tf_op jit(solution)/shard_map/reduce_scatter | solution.py:64
Sparse Core Ops, SparseCore 0:
  22.2 72.6 all-gather.4
  97.0 70.4 all-gather.2
  381.1 108.0 reduce-scatter.2
  492.0 31.2 reduce-scatter.4
where the time goes:
time: 530 us
  waiting for transfers between devices  253 us (48%)
  blocking collectives  221 us (42%)
  matrix products  40.8 us (8%)
  between operations  13.8 us (3%)
    reduce_scatter x1, waiting for transfers between devices, shards(): lax.psum_scatter(jnp.dot(grad_logits, w_policy, preferred_element_type=jn...  108 us
    pmax x1, blocking collectives, shards(): lax.pmax((jnp.max(logits, axis=1), jnp.max(ref_logits, axis=1)), ('sectio...  64.5 us
    psum x1, blocking collectives, shards(): lax.psum((jnp.sum(jnp.exp(logits - maximum[:, None]), axis=1), jnp.sum(jn...  64.3 us
    all_gather x1, waiting for transfers between devices, shards(): full_hidden = lax.all_gather(features, 'section', axis=0, tiled=True)  63.1 us
    psum x1, blocking collectives, shards(): lax.psum(jnp.sum(probabilities * (log_probs - ref_log_probs), axis=1), ('...  62.4 us
    all_gather x1, waiting for transfers between devices, shards(): lax.all_gather(ref_features, 'section', axis=0, tiled=True)  57.6 us
    reduce_scatter x1, waiting for transfers between devices, shards(): lax.psum_scatter(row_terms, 'tensor', scatter_dimension=1, tiled=True)  23.7 us
    all_gather x1, blocking collectives, shards(): lax.all_gather(ref_hidden, 'tensor', axis=1, tiled=True)  14.9 us
  transfers between devices with their start and end apart: 4, of which 4 were waited for; matrix products, arithmetic and copies ran while one was open for 4% of the time, Pallas kernels for 0%

commit v1 on v0

v1 whole, which is shorter than its diff:
```python
import functools

import jax
import jax.numpy as jnp
from jax import lax
from jax.experimental import pallas as pl
from jax.experimental.pallas import tpu as pltpu
from jax.sharding import PartitionSpec as P

MESH = pl.DeviceIdType.MESH
bf16, f32 = jnp.bfloat16, jnp.float32

loss_scale = 4.0
penalty_weight = 0.2

R = 16
H = 2
WIDTH = 1024
T = 16 * R
VW = 512
X, Y, Z = 0, 1, 2
ORDERS = ((X, Y, Z), (Y, Z, X), (Z, X, Y))
GATHER_COLS = (((0, 768), (768, 640), (1408, 640)), ((0, 640), (640, 640), (1280, 768)))
REDUCE_COLS = (((0, 384), (384, 384), (768, 256)), ((0, 384), (384, 256), (640, 384)))
ALL = slice(None)
LOW, HIGH = slice(0, 2), slice(2, 4)


def wrap(i):
    return lax.rem(i + 4, 4)


def pick(ref, lead, axes, where, cols):
    index = tuple(lead)
    for axis in axes:
        index += (where.get(axis, ALL),)
    return ref.at[index + (ALL, pl.ds(*cols))]


def kernel(
    hid, rhid, w_hbm, wr_hbm, tok, out_h, out_w,
    g, w, wr, lg, rlg, gv, gt, st_s, st_r,
    ysend, yrecv, s, fw, rl, rr, t3, fw2, rl2, rr2, t2, r1,
    load_sem, ag_send, ag_recv, dd_send, dd_recv, st_send, st_recv,
    y_send, y_recv, rs_send, rs_recv, out_sem,
):
    section, tensor = lax.axis_index("section"), lax.axis_index("tensor")
    x, c = tensor // 2, lax.rem(tensor, 2)
    y, z = section // 4, lax.rem(section, 4)
    me = (x, y, z)
    offset = (section * 8 + tensor) * VW

    def device(dx=0, dy=0, dz=0, dc=0):
        return (
            lax.rem(y + dy + 4, 4) * 4 + lax.rem(z + dz + 4, 4),
            lax.rem(x + dx + 4, 4) * 2 + lax.rem(c + dc, 2),
        )

    def along(axis, k):
        step = [0, 0, 0]
        step[axis] = k
        return device(*step)

    def send(src, dst, ssem, rsem, to):
        pltpu.make_async_remote_copy(
            src_ref=src, dst_ref=dst, send_sem=ssem, recv_sem=rsem, device_id=to, device_id_type=MESH
        ).start()

    def wait(ref, sem):
        pltpu.make_async_copy(ref, ref, sem).wait()

    tensor_peers = [(kx, kc) for kx in range(4) for kc in range(2) if (kx, kc) != (0, 0)]
    peers = [dict(dx=kx, dc=kc) for kx, kc in tensor_peers]
    peers += [dict(dy=k) for k in (1, 2, 3)] + [dict(dz=k) for k in (1, 2, 3)]

    loads = [
        pltpu.make_async_copy(
            src.at[pl.ds(h * R, R), :],
            g.at[h, c, x, y, z, :, pl.ds(m * WIDTH, WIDTH)],
            load_sem.at[2 * h + m],
        )
        for h in range(H)
        for m, src in enumerate((hid, rhid))
    ]
    for copy in loads:
        copy.start()
    weight_loads = [
        pltpu.make_async_copy(w_hbm, w, load_sem.at[4]),
        pltpu.make_async_copy(wr_hbm, wr, load_sem.at[5]),
    ]
    barrier = pltpu.get_barrier_semaphore()
    for peer in peers:
        pl.semaphore_signal(barrier, inc=1, device_id=device(**peer), device_id_type=MESH)
    for copy in loads:
        copy.wait()
    pl.semaphore_wait(barrier, len(peers))

    def ag_part(h, r, where):
        return pick(g, (h, c), (X, Y, Z), where, GATHER_COLS[h][r])

    def ag_send_part(h, r, where, axis, k, event):
        part = ag_part(h, r, where)
        send(part, part, ag_send.at[h], ag_recv.at[h, r, event], along(axis, k))

    def ag_core(h, r, where):
        part = ag_part(h, r, where)
        send(part, part, dd_send.at[h], dd_recv.at[h], device(dc=1))

    def ag_wait(h, r, event, where):
        wait(ag_part(h, r, where), ag_recv.at[h, r, event])

    one_line, two_lines, four_lines = {X: 0, Y: 0}, {X: 0, Y: slice(0, 2)}, {X: 0}

    def ag0(h):
        for r, (a1, a2, a3) in enumerate(ORDERS):
            for k in (1, 3, 2):
                ag_send_part(h, r, {a1: me[a1], a2: me[a2], a3: me[a3]}, a1, k, 0)

    def ag1(h):
        for r, (a1, a2, a3) in enumerate(ORDERS):
            ag_wait(h, r, 0, {X: 0, Y: 0, Z: slice(0, 3)})
            line = {a2: me[a2], a3: me[a3]}
            for k in (1, 3):
                ag_send_part(h, r, line, a2, k, 1)
            for k in (1, 3):
                ag_send_part(h, r, line, a3, k, 3)
            ag_core(h, r, line)

    def ag2(h):
        for r, (a1, a2, a3) in enumerate(ORDERS):
            m2, m3 = me[a2], me[a3]
            ag_wait(h, r, 1, two_lines)
            left, right = wrap(m2 - 1), wrap(m2 + 1)
            ag_send_part(h, r, {a1: LOW, a2: left, a3: m3}, a2, 1, 2)
            ag_send_part(h, r, {a1: HIGH, a2: right, a3: m3}, a2, 3, 2)
            for j in (left, right):
                for k in (1, 3):
                    ag_send_part(h, r, {a2: j, a3: m3}, a3, k, 4)
                ag_core(h, r, {a2: j, a3: m3})

    def ag_last(h, r, lines, event, waited):
        a1, a2, a3 = ORDERS[r]
        left, right = wrap(me[a3] - 1), wrap(me[a3] + 1)
        ag_wait(h, r, event, waited)
        for j in lines:
            ag_send_part(h, r, {a1: LOW, a2: j, a3: left}, a3, 1, 6)
            ag_send_part(h, r, {a1: HIGH, a2: j, a3: right}, a3, 3, 6)
        for j in lines:
            ag_core(h, r, {a2: j, a3: left})
            ag_core(h, r, {a2: j, a3: right})

    def ag3(h):
        for r, (a1, a2, a3) in enumerate(ORDERS):
            ag_last(h, r, (me[a2],), 3, two_lines)

    def ag4(h):
        for r, (a1, a2, a3) in enumerate(ORDERS):
            ag_wait(h, r, 2, one_line)
            line = {a2: wrap(me[a2] + 2), a3: me[a3]}
            for k in (1, 3):
                ag_send_part(h, r, line, a3, k, 5)
            ag_core(h, r, line)

    def ag5(h):
        for r, (a1, a2, a3) in enumerate(ORDERS):
            ag_last(h, r, (wrap(me[a2] - 1), wrap(me[a2] + 1)), 4, four_lines)

    def ag6(h):
        for r, (a1, a2, a3) in enumerate(ORDERS):
            ag_last(h, r, (wrap(me[a2] + 2),), 5, two_lines)

    def ag7(h):
        for r, (a1, a2, a3) in enumerate(ORDERS):
            ag_wait(h, r, 6, four_lines)
            ag_core(h, r, {a3: wrap(me[a3] + 2)})

    def ag_core_wait(h):
        wait(g.at[h, 1 - c], dd_recv.at[h])

    def logits(h, core, first, last):
        def step(i, carry):
            column = pl.multiple_of((i * 2 + core) * WIDTH, WIDTH)
            for m, (weights, acc) in enumerate(((w, lg), (wr, rlg))):
                rows = g[h, core, i, :, :, :, m * WIDTH:(m + 1) * WIDTH].reshape(T, WIDTH)
                acc[h] += lax.dot_general(
                    weights[:, pl.ds(column, WIDTH)], rows, (((1,), (1,)), ((), ())), preferred_element_type=f32
                )
            return carry

        lax.fori_loop(first, last, step, 0)

    def clear(h):
        lg[h] = jnp.zeros((VW, T), f32)
        rlg[h] = jnp.zeros((VW, T), f32)

    def local_stats(h):
        l, rf = lg[h], rlg[h]
        m = jnp.max(l, axis=0, keepdims=True)
        rm = jnp.max(rf, axis=0, keepdims=True)
        lm, rfm = l - m, rf - rm
        e = jnp.exp(lm)
        mass = jnp.sum(e, axis=0, keepdims=True)
        rmass = jnp.sum(jnp.exp(rfm), axis=0, keepdims=True)
        d = jnp.sum(e * (lm - rfm), axis=0, keepdims=True)
        st_s[h, 0] = jnp.concatenate([m, mass, rm, rmass, d, d, d, d], axis=0)

    groups = (
        [dict(dx=kx, dc=kc) for kx, kc in tensor_peers],
        [dict(dy=k) for k in (1, 2, 3)],
        [dict(dz=k) for k in (1, 2, 3)],
    )
    starts = (0, 7, 10)

    def stats_send(h, phase):
        for i, peer in enumerate(groups[phase]):
            send(
                st_s.at[h, phase], st_r.at[h, starts[phase] + i],
                st_send.at[h, phase], st_recv.at[h, phase], device(**peer),
            )

    def stats_wait(h, phase):
        n = len(groups[phase])
        wait(st_r.at[h, pl.ds(starts[phase], n)], st_recv.at[h, phase])
        terms = [st_s[h, phase]] + [st_r[h, starts[phase] + i] for i in range(n)]
        m = functools.reduce(jnp.maximum, [a[0:1] for a in terms])
        rm = functools.reduce(jnp.maximum, [a[2:3] for a in terms])
        mass, rmass, d = 0.0, 0.0, 0.0
        for a in terms:
            dm, drm = a[0:1] - m, a[2:3] - rm
            scale = jnp.exp(dm)
            mass += scale * a[1:2]
            rmass += jnp.exp(drm) * a[3:4]
            d += scale * (a[4:5] + a[1:2] * (dm - drm))
        st_s[h, phase + 1] = jnp.concatenate([m, mass, rm, rmass, d, d, d, d], axis=0)

    def grads(h):
        a = st_s[h, 3]
        m, mass, rm, rmass, d = a[0:1], a[1:2], a[2:3], a[3:4], a[4:5]
        ln, rln = jnp.log(mass), jnp.log(rmass)
        divergence = d / mass - ln + rln
        ids, mask, adv = tok[h, 0:1], tok[h, 1:2], tok[h, 2:3]
        weight = loss_scale * mask
        place = ids - offset.astype(f32)

        def step(i, carry):
            rows = pl.multiple_of(i * 128, 128)
            lp = (lg[h, pl.ds(rows, 128), :] - m) - ln
            rlp = (rlg[h, pl.ds(rows, 128), :] - rm) - rln
            p = jnp.exp(lp)
            entry = (rows + lax.broadcasted_iota(jnp.int32, (128, T), 0)).astype(f32)
            target = (entry == place).astype(f32)
            value = weight * (adv * (p - target) + penalty_weight * p * (lp - rlp - divergence))
            gv[pl.ds(rows, 128), h * T:(h + 1) * T] = value.astype(bf16)
            gt[h, :, pl.ds(rows, 128)] = value.T.astype(bf16)
            return carry

        lax.fori_loop(0, VW // 128, step, 0)

    def products_other(h):
        for i in range(4):
            column = pl.multiple_of((i * 2 + 1 - c) * WIDTH, WIDTH)
            rows = jnp.dot(gt[h], w[:, pl.ds(column, WIDTH)], preferred_element_type=f32)
            ysend[h, i] = rows.astype(bf16).reshape(4, 4, R, WIDTH)
            send(ysend.at[h, i], yrecv.at[h, i], y_send.at[h], y_recv.at[h, i], device(dc=1))

    def products_own(h):
        for i in range(4):
            column = pl.multiple_of((i * 2 + c) * WIDTH, WIDTH)
            rows = jnp.dot(gt[h], w[:, pl.ds(column, WIDTH)], preferred_element_type=f32)
            wait(yrecv.at[h, i], y_recv.at[h, i])
            rows += yrecv[h, i].reshape(T, WIDTH).astype(f32)
            s[h, i] = rows.astype(bf16).reshape(4, 4, R, WIDTH)

    def rs_axes(r):
        a1, a2, a3 = ORDERS[r]
        plane = tuple(a for a in (X, Y, Z) if a != a3)
        return a1, a2, a3, plane

    def rs3_start(h):
        for r in range(3):
            a1, a2, a3, plane = rs_axes(r)
            m3, cols = me[a3], REDUCE_COLS[h][r]
            at = lambda ref, where: pick(ref, (h,), plane, where, cols)
            mine = lambda where: pick(s, (h,), (X, Y, Z), where, cols)
            right, left, far = wrap(m3 + 1), wrap(m3 - 1), wrap(m3 + 2)
            ss = rs_send.at[h, 0]
            send(mine({a1: LOW, a3: far}), at(fw, {a1: LOW}), ss, rs_recv.at[h, r, 0], along(a3, 1))
            send(mine({a1: HIGH, a3: far}), at(fw, {a1: HIGH}), ss, rs_recv.at[h, r, 0], along(a3, 3))
        for r in range(3):
            a1, a2, a3, plane = rs_axes(r)
            m3, cols = me[a3], REDUCE_COLS[h][r]
            at = lambda ref, where: pick(ref, (h,), plane, where, cols)
            mine = lambda where: pick(s, (h,), (X, Y, Z), where, cols)
            right, left = wrap(m3 + 1), wrap(m3 - 1)
            ss = rs_send.at[h, 0]
            send(mine({a1: HIGH, a3: right}), at(rl, {a1: HIGH}), ss, rs_recv.at[h, r, 1], along(a3, 1))
            send(mine({a1: LOW, a3: left}), at(rr, {a1: LOW}), ss, rs_recv.at[h, r, 1], along(a3, 3))

    def rs3_middle(h):
        for r in range(3):
            a1, a2, a3, plane = rs_axes(r)
            m3, cols = me[a3], REDUCE_COLS[h][r]
            at = lambda ref, where: pick(ref, (h,), plane, where, cols)
            mine = lambda where: pick(s, (h,), (X, Y, Z), where, cols)
            wait(at(fw, {}), rs_recv.at[h, r, 0])
            for part, to, k, dst in ((LOW, wrap(m3 + 1), 1, rl), (HIGH, wrap(m3 - 1), 3, rr)):
                place = at(fw, {a1: part})
                place[...] = (place[...].astype(f32) + mine({a1: part, a3: to})[...].astype(f32)).astype(bf16)
                send(place, at(dst, {a1: part}), rs_send.at[h, 0], rs_recv.at[h, r, 2], along(a3, k))

    def rs3_end(h):
        for r in range(3):
            a1, a2, a3, plane = rs_axes(r)
            m3, m2, cols = me[a3], me[a2], REDUCE_COLS[h][r]
            at = lambda ref, where: pick(ref, (h,), plane, where, cols)
            mine = lambda where: pick(s, (h,), (X, Y, Z), where, cols)
            line = lambda ref, where: pick(ref, (h,), (a1,), where, cols)
            wait(at(rl, {}), rs_recv.at[h, r, 1])
            wait(at(rr, {}), rs_recv.at[h, r, 2])
            total = mine({a3: m3})[...].astype(f32) + at(rl, {})[...].astype(f32) + at(rr, {})[...].astype(f32)
            at(t3, {})[...] = total.astype(bf16)
            far, right, left = wrap(m2 + 2), wrap(m2 + 1), wrap(m2 - 1)
            ss = rs_send.at[h, 1]
            send(at(t3, {a1: LOW, a2: far}), line(fw2, {a1: LOW}), ss, rs_recv.at[h, r, 3], along(a2, 1))
            send(at(t3, {a1: HIGH, a2: far}), line(fw2, {a1: HIGH}), ss, rs_recv.at[h, r, 3], along(a2, 3))
            send(at(t3, {a1: HIGH, a2: right}), line(rl2, {a1: HIGH}), ss, rs_recv.at[h, r, 4], along(a2, 1))
            send(at(t3, {a1: LOW, a2: left}), line(rr2, {a1: LOW}), ss, rs_recv.at[h, r, 4], along(a2, 3))

    def rs2_middle(h):
        for r in range(3):
            a1, a2, a3, plane = rs_axes(r)
            m2, cols = me[a2], REDUCE_COLS[h][r]
            at = lambda ref, where: pick(ref, (h,), plane, where, cols)
            line = lambda ref, where: pick(ref, (h,), (a1,), where, cols)
            wait(line(fw2, {}), rs_recv.at[h, r, 3])
            for part, to, k, dst in ((LOW, wrap(m2 + 1), 1, rl2), (HIGH, wrap(m2 - 1), 3, rr2)):
                place = line(fw2, {a1: part})
                place[...] = (place[...].astype(f32) + at(t3, {a1: part, a2: to})[...].astype(f32)).astype(bf16)
                send(place, line(dst, {a1: part}), rs_send.at[h, 1], rs_recv.at[h, r, 5], along(a2, k))

    def rs2_end(h):
        for r in range(3):
            a1, a2, a3, plane = rs_axes(r)
            m1, m2, cols = me[a1], me[a2], REDUCE_COLS[h][r]
            at = lambda ref, where: pick(ref, (h,), plane, where, cols)
            line = lambda ref, where: pick(ref, (h,), (a1,), where, cols)
            wait(line(rl2, {}), rs_recv.at[h, r, 4])
            wait(line(rr2, {}), rs_recv.at[h, r, 5])
            total = at(t3, {a2: m2})[...].astype(f32) + line(rl2, {})[...].astype(f32)
            line(t2, {})[...] = total + line(rr2, {})[...].astype(f32)
            for k in (1, 2, 3):
                send(
                    line(t2, {a1: wrap(m1 + k)}), pick(r1, (h,), (a1,), {a1: k - 1}, cols),
                    rs_send.at[h, 2], rs_recv.at[h, r, 6], along(a1, k),
                )

    def rs1_end(h):
        for r in range(3):
            a1, a2, a3, plane = rs_axes(r)
            cols = REDUCE_COLS[h][r]
            wait(pick(r1, (h,), (a1,), {}, cols), rs_recv.at[h, r, 6])
            total = pick(t2, (h,), (a1,), {a1: me[a1]}, cols)[...]
            for k in range(3):
                total += pick(r1, (h,), (a1,), {a1: k}, cols)[...]
            out_h[h * R:(h + 1) * R, cols[0]:cols[0] + cols[1]] = total

    def head(first, last):
        def step(i, carry):
            core, col = lax.rem(i, 2), i // 2
            column = pl.multiple_of(i * WIDTH, WIDTH)
            total = 0.0
            for h in range(H):
                rows = g[h, core, col, :, :, :, 0:WIDTH].reshape(T, WIDTH)
                total += jnp.dot(gv[:, h * T:(h + 1) * T], rows, preferred_element_type=f32)
            wr[:, pl.ds(column, WIDTH)] = total.astype(bf16)
            pltpu.make_async_copy(
                wr.at[:, pl.ds(column, WIDTH)], out_w.at[:, pl.ds(column, WIDTH)], out_sem
            ).start()
            return carry

        lax.fori_loop(first, last, step, 0)

    ag0(0)
    for copy in weight_loads:
        copy.start()
    clear(0)
    clear(1)
    ag1(0)
    ag0(1)
    ag2(0)
    ag3(0)
    ag1(1)
    ag4(0)
    ag5(0)
    ag2(1)
    ag6(0)
    ag3(1)
    ag7(0)
    for copy in weight_loads:
        copy.wait()
    logits(0, c, 0, 2)
    ag4(1)
    logits(0, c, 2, 4)
    ag5(1)
    ag_core_wait(0)
    logits(0, 1 - c, 0, 4)
    ag6(1)
    local_stats(0)
    stats_send(0, 0)
    stats_wait(0, 0)
    stats_send(0, 1)
    stats_wait(0, 1)
    stats_send(0, 2)
    ag7(1)
    stats_wait(0, 2)
    grads(0)
    products_other(0)
    products_own(0)
    rs3_start(0)
    logits(1, c, 0, 4)
    ag_core_wait(1)
    logits(1, 1 - c, 0, 2)
    rs3_middle(0)
    logits(1, 1 - c, 2, 4)
    local_stats(1)
    stats_send(1, 0)
    stats_wait(1, 0)
    stats_send(1, 1)
    rs3_end(0)
    stats_wait(1, 1)
    stats_send(1, 2)
    rs2_middle(0)
    stats_wait(1, 2)
    grads(1)
    products_other(1)
    products_own(1)
    rs3_start(1)
    rs2_end(0)
    head(0, 4)
    rs3_middle(1)
    rs1_end(0)
    head(4, 8)
    rs3_end(1)
    rs2_middle(1)
    rs2_end(1)
    rs1_end(1)

    wait(wr, out_sem)
    for h in range(H):
        wait(w.at[pl.ds(0, 256), pl.ds(0, 63 * 128)], ag_send.at[h])
        wait(g.at[h, c], dd_send.at[h])
        for phase in range(3):
            n = len(groups[phase])
            wait(st_r.at[h, pl.ds(starts[phase], n)], st_send.at[h, phase])
        wait(ysend.at[h], y_send.at[h])
        wait(s.at[h, pl.ds(0, 3)], rs_send.at[h, 0])
        wait(s.at[h, 0, pl.ds(0, 3)], rs_send.at[h, 1])
        wait(t2.at[h, pl.ds(0, 3)], rs_send.at[h, 2])


def shards(hidden, ref_hidden, w_policy, w_ref, token_ids, loss_mask, advantages):
    by_half = lambda a: a.astype(f32).reshape(16, H, R).transpose(1, 0, 2).reshape(H, 1, T)
    tok = jnp.concatenate([by_half(token_ids), by_half(loss_mask), by_half(advantages)], axis=1)
    tok = jnp.pad(tok, ((0, 0), (0, 5), (0, 0)))
    any_space = pl.BlockSpec(memory_space=pl.ANY)
    vmem = pl.BlockSpec(memory_space=pltpu.VMEM)
    dma = pltpu.SemaphoreType.DMA
    return pl.pallas_call(
        kernel,
        out_shape=(
            jax.ShapeDtypeStruct((H * R, WIDTH), f32),
            jax.ShapeDtypeStruct((VW, 8 * WIDTH), bf16),
        ),
        in_specs=[any_space] * 4 + [vmem],
        out_specs=(vmem, any_space),
        scratch_shapes=[
            pltpu.VMEM((H, 2, 4, 4, 4, R, 2 * WIDTH), bf16),
            pltpu.VMEM((VW, 8 * WIDTH), bf16),
            pltpu.VMEM((VW, 8 * WIDTH), bf16),
            pltpu.VMEM((H, VW, T), f32),
            pltpu.VMEM((H, VW, T), f32),
            pltpu.VMEM((VW, H * T), bf16),
            pltpu.VMEM((H, T, VW), bf16),
            pltpu.VMEM((H, 4, 8, T), f32),
            pltpu.VMEM((H, 13, 8, T), f32),
            pltpu.VMEM((H, 4, 4, 4, R, WIDTH), bf16),
            pltpu.VMEM((H, 4, 4, 4, R, WIDTH), bf16),
            pltpu.VMEM((H, 4, 4, 4, R, WIDTH), bf16),
            pltpu.VMEM((H, 4, 4, R, WIDTH), bf16),
            pltpu.VMEM((H, 4, 4, R, WIDTH), bf16),
            pltpu.VMEM((H, 4, 4, R, WIDTH), bf16),
            pltpu.VMEM((H, 4, 4, R, WIDTH), bf16),
            pltpu.VMEM((H, 4, R, WIDTH), bf16),
            pltpu.VMEM((H, 4, R, WIDTH), bf16),
            pltpu.VMEM((H, 4, R, WIDTH), bf16),
            pltpu.VMEM((H, 4, R, WIDTH), f32),
            pltpu.VMEM((H, 3, R, WIDTH), f32),
            dma((6,)),
            dma((H,)),
            dma((H, 3, 7)),
            dma((H,)),
            dma((H,)),
            dma((H, 3)),
            dma((H, 3)),
            dma((H,)),
            dma((H, 4)),
            dma((H, 3)),
            dma((H, 3, 7)),
            dma,
        ],
        compiler_params=pltpu.CompilerParams(
            collective_id=0, has_side_effects=True, vmem_limit_bytes=62 * 2**20
        ),
        cost_estimate=pl.CostEstimate(flops=4 * 2 * 512 * 512 * 8192, bytes_accessed=3 * 2**23, transcendentals=2**20),
        name="head_step",
    )(hidden, ref_hidden, w_policy, w_ref, tok)


def solution(mesh):
    placed = (
        P("section", "tensor"),
        P("section", "tensor"),
        P(("section", "tensor"), None),
        P(("section", "tensor"), None),
        P(),
        P(),
        P(),
    )
    return jax.shard_map(
        shards,
        mesh=mesh,
        in_specs=placed,
        out_specs=(P("section", "tensor"), P(("section", "tensor"), None)),
        check_vma=False,
    )
```

time: 530 us -> 119 us (0.22)
  waiting for transfers between devices: 253 us -> 0 us
  blocking collectives: 221 us -> 0 us
  Pallas kernels: 0 us -> 105 us
  matrix products: 40.8 us -> 0 us
  between operations: 13.8 us -> 0.68 us
  local copies, waits for them, and re-layouts: 0.01 us -> 10.5 us
    reduce_scatter x2 -> x0, waiting for transfers between devices: 132 us -> none  [the longest x1 108 us: shards(): lax.psum_scatter(jnp.dot(grad_logits, w_policy, preferred_element_type=jn...]
    psum x2 -> x0, blocking collectives: 127 us -> none  [the longest x1 64.3 us: shards(): lax.psum((jnp.sum(jnp.exp(logits - maximum[:, None]), axis=1), jnp.sum(jn...]
    all_gather x2 -> x0, waiting for transfers between devices: 121 us -> none  [the longest x1 63.1 us: shards(): full_hidden = lax.all_gather(features, 'section', axis=0, tiled=True)]
    pallas_call x0 -> x1, Pallas kernels: none -> 105 us  [shards(): pl.pallas_call(kernel, out_shape=(jax.ShapeDtypeStruct((H * R, WIDTH), f3...]
    pmax x1 -> x0, blocking collectives: 64.5 us -> none  [shards(): lax.pmax((jnp.max(logits, axis=1), jnp.max(ref_logits, axis=1)), ('sectio...]
    dot_general x4 -> x0, matrix products: 40.8 us -> none  [the longest x1 11.5 us: shards(): jnp.dot(grad_logits, w_policy, preferred_element_type=jnp.float32)]
    all_gather x2 -> x0, blocking collectives: 29.3 us -> none  [the longest x1 14.9 us: shards(): lax.all_gather(ref_hidden, 'tensor', axis=1, tiled=True)]
    unnamed x4 -> x2, local copies, waits for them, and re-layouts: 0.01 us -> 9.34 us
  transfers between devices with their start and end apart: 4 -> 0, of which waited for: 4 -> 0; matrix products, arithmetic and copies ran while one was open for 4% -> 0% of each run, Pallas kernels for 0% -> 0%
where the time goes in v1:
time: 119 us
  Pallas kernels  105 us (88%)
  local copies, waits for them, and re-layouts  10.5 us (9%)
  other arithmetic  1.99 us (2%)
    pallas_call x1, Pallas kernels, shards(): pl.pallas_call(kernel, out_shape=(jax.ShapeDtypeStruct((H * R, WIDTH), f3...  105 us
    unnamed x2, local copies, waits for them, and re-layouts  9.34 us

profile of v1, /device:TPU:0, one launch (start us, length us, event | category | flops | bytes accessed | tf_op | source)
XLA Modules:
  0.0 118.6 jit_solution(14230959037456125517)
XLA Ops:
  0.6 0.7 convert_element_type.8
  1.3 0.7 convert_element_type.9
  2.0 0.1 reshape.24
  2.1 0.1 reshape.25
  2.2 0.1 reshape.22
  2.3 0.1 reshape.23
  2.4 0.8 reshape.26
  3.2 0.1 reshape.27
  3.2 0.6 select_maximum_fusion.tok
  3.9 105.4 %head_step.1 = (f32[32,1024]{1,0:T(8,128)}, bf16[512,8192]{1,0:T(8,128)(2,1)}) custom-call(bf16[32,1024]{1,0:T(8,128)(2,1)} %hid.1, bf16[32,1024]{1,0:T(8,128)(2,1)} %rhid.1, bf16[512,8192]{1,0:T(8,128)(2,1)} %w_hbm.1, bf16[512,8192]{1,0:T(8,128)(2,1)} %wr_hbm.1, f32[2,8,256]{2,1,0:T(8,128)} %select_maximum_fusion.tok), custom_call_target="tpu_custom_call" | custom-call | flops 17179869184 | bytes 25165824 | tf_op jit(solution)/shard_map/head_step/pallas_call | solution.py:468
  109.3 1.6 %copy.14 = f32[32,1024]{1,0:T(8,128)} copy(f32[32,1024]{1,0:T(8,128)} %get-tuple-element.4) | data formatting | bytes 262144
  110.9 7.8 %copy.15 = bf16[512,8192]{1,0:T(8,128)(2,1)} copy(bf16[512,8192]{1,0:T(8,128)(2,1)} %get-tuple-element.5) | data formatting | bytes 16777216
  (3 shorter events, 0.0 us)

commit v2 on v0

v2 whole, which is shorter than its diff:
```python
import functools

import jax
import jax.numpy as jnp
from jax import lax
from jax.experimental import pallas as pl
from jax.experimental.pallas import tpu as pltpu
from jax.sharding import PartitionSpec as P

MESH = pl.DeviceIdType.MESH
bf16, f32 = jnp.bfloat16, jnp.float32

loss_scale = 4.0
penalty_weight = 0.2

R = 32
WIDTH = 1024
T = 16 * R
VW = 512
X, Y, Z = 0, 1, 2
ORDERS = ((X, Y, Z), (Y, Z, X), (Z, X, Y))
GATHER = (
    ((0, 0, 32, 0, 384), (1, 0, 32, 384, 384), (2, 0, 32, 768, 256)),
    ((0, 0, 32, 1024, 256), (1, 0, 32, 1280, 256), (2, 0, 32, 1536, 384), (0, 0, 16, 1920, 128), (1, 16, 16, 1920, 128)),
)
REDUCE = ((0, 0, 32, 0, 256), (1, 0, 32, 256, 384), (2, 0, 32, 640, 384))
ROUNDS, PARTS = 2, 5
ALL = slice(None)
LOW, HIGH = slice(0, 2), slice(2, 4)


def wrap(i):
    return lax.rem(i + 4, 4)


def pick(ref, lead, axes, where, part):
    index = tuple(lead)
    for axis in axes:
        index += (where.get(axis, ALL),)
    return ref.at[index + (pl.ds(part[1], part[2]), pl.ds(part[3], part[4]))]


def kernel(
    hid, rhid, w_hbm, wr_hbm, ids_ref, mask_ref, adv_ref, out_h, out_w,
    g, w, wr, lg, rlg, gv, gt, st_s, st_r,
    fw, rl, rr, t3, fw2, rl2, rr2, t2, r1,
    load_sem, ag_send, ag_recv, dd_send, dd_recv, st_send, st_recv,
    y_send, y_recv, rs_send, rs3, rs2, rs1,
):
    section, tensor = lax.axis_index("section"), lax.axis_index("tensor")
    x, c = tensor // 2, lax.rem(tensor, 2)
    y, z = section // 4, lax.rem(section, 4)
    me = (x, y, z)
    offset = (section * 8 + tensor) * VW

    def device(dx=0, dy=0, dz=0, dc=0):
        return (
            lax.rem(y + dy + 4, 4) * 4 + lax.rem(z + dz + 4, 4),
            lax.rem(x + dx + 4, 4) * 2 + lax.rem(c + dc, 2),
        )

    def along(axis, k):
        step = [0, 0, 0]
        step[axis] = k
        return device(*step)

    def send(src, dst, ssem, rsem, to):
        pltpu.make_async_remote_copy(
            src_ref=src, dst_ref=dst, send_sem=ssem, recv_sem=rsem, device_id=to, device_id_type=MESH
        ).start()

    def wait(ref, sem):
        pltpu.make_async_copy(ref, ref, sem).wait()

    tensor_peers = [(kx, kc) for kx in range(4) for kc in range(2) if (kx, kc) != (0, 0)]
    groups = (
        [dict(dx=kx, dc=kc) for kx, kc in tensor_peers],
        [dict(dy=ky, dz=kz) for ky in range(4) for kz in range(4) if (ky, kz) != (0, 0)],
    )
    starts = (0, 7)
    peers = [peer for group in groups for peer in group]

    loads = [
        pltpu.make_async_copy(src, g.at[c, x, y, z, :, pl.ds(m * WIDTH, WIDTH)], load_sem.at[m])
        for m, src in enumerate((hid, rhid))
    ]
    for copy in loads:
        copy.start()
    barrier = pltpu.get_barrier_semaphore()
    for peer in peers:
        pl.semaphore_signal(barrier, inc=1, device_id=device(**peer), device_id_type=MESH)
    for copy in loads:
        copy.wait()
    pl.semaphore_wait(barrier, len(peers))

    def weights_start():
        for i in range(8):
            cols = pl.ds(i * WIDTH, WIDTH)
            pltpu.make_async_copy(w_hbm.at[:, cols], w.at[i], load_sem.at[2]).start()
        for i in range(8):
            cols = pl.ds(i * WIDTH, WIDTH)
            pltpu.make_async_copy(wr_hbm.at[:, :, :, cols], wr.at[i], load_sem.at[3]).start()

    def ag_part(part, where):
        return pick(g, (c,), (X, Y, Z), where, part)

    def ag_send_part(q, i, where, axis, k, event):
        part = ag_part(GATHER[q][i], where)
        send(part, part, ag_send, ag_recv.at[q, i, event], along(axis, k))

    def ag_core(q, i, where):
        part = ag_part(GATHER[q][i], where)
        send(part, part, dd_send, dd_recv.at[q], device(dc=1))

    def ag_wait(q, i, event, where):
        wait(ag_part(GATHER[q][i], where), ag_recv.at[q, i, event])

    def parts_of(q):
        return [(i,) + ORDERS[part[0]] for i, part in enumerate(GATHER[q])]

    one_line, two_lines, four_lines = {X: 0, Y: 0}, {X: 0, Y: slice(0, 2)}, {X: 0}

    def ag0(q):
        for i, a1, a2, a3 in parts_of(q):
            for k in (1, 3, 2):
                ag_send_part(q, i, {a1: me[a1], a2: me[a2], a3: me[a3]}, a1, k, 0)
            for axis, event in ((a2, 1), (a3, 3)):
                for k in (1, 3):
                    ag_send_part(q, i, {a1: me[a1], a2: me[a2], a3: me[a3]}, axis, k, event)

    def ag1(q):
        for i, a1, a2, a3 in parts_of(q):
            ag_wait(q, i, 0, {X: 0, Y: 0, Z: slice(0, 3)})
            line = {a2: me[a2], a3: me[a3]}
            for j in (1, 3, 2):
                block = {a1: wrap(me[a1] + j), **line}
                for axis, event in ((a2, 1), (a3, 3)):
                    for k in (1, 3):
                        ag_send_part(q, i, block, axis, k, event)

    def ag2(q):
        for i, a1, a2, a3 in parts_of(q):
            m2, m3 = me[a2], me[a3]
            ag_wait(q, i, 1, two_lines)
            left, right = wrap(m2 - 1), wrap(m2 + 1)
            ag_send_part(q, i, {a1: LOW, a2: left, a3: m3}, a2, 1, 2)
            ag_send_part(q, i, {a1: HIGH, a2: right, a3: m3}, a2, 3, 2)
            for j in (left, right):
                for k in (1, 3):
                    ag_send_part(q, i, {a2: j, a3: m3}, a3, k, 4)

    def ag_last(q, i, lines, event, waited):
        a1, a2, a3 = ORDERS[GATHER[q][i][0]]
        left, right = wrap(me[a3] - 1), wrap(me[a3] + 1)
        ag_wait(q, i, event, waited)
        for j in lines:
            ag_send_part(q, i, {a1: LOW, a2: j, a3: left}, a3, 1, event + 3)
            ag_send_part(q, i, {a1: HIGH, a2: j, a3: right}, a3, 3, event + 3)
        for j in lines:
            ag_core(q, i, {a2: j, a3: left})
            ag_core(q, i, {a2: j, a3: right})

    def ag3(q):
        for i, a1, a2, a3 in parts_of(q):
            ag_last(q, i, (me[a2],), 3, two_lines)

    def ag4(q):
        for i, a1, a2, a3 in parts_of(q):
            ag_wait(q, i, 2, one_line)
            line = {a2: wrap(me[a2] + 2), a3: me[a3]}
            for k in (1, 3):
                ag_send_part(q, i, line, a3, k, 5)
            ag_core(q, i, {a3: me[a3]})

    def ag5(q):
        for i, a1, a2, a3 in parts_of(q):
            ag_last(q, i, (wrap(me[a2] - 1), wrap(me[a2] + 1)), 4, four_lines)

    def ag6(q):
        for i, a1, a2, a3 in parts_of(q):
            ag_last(q, i, (wrap(me[a2] + 2),), 5, two_lines)

    def ag7(q):
        for i, a1, a2, a3 in parts_of(q):
            far = wrap(me[a3] + 2)
            ag_wait(q, i, 6, one_line)
            ag_core(q, i, {a2: me[a2], a3: far})
            ag_wait(q, i, 7, two_lines)
            ag_core(q, i, {a2: wrap(me[a2] - 1), a3: far})
            ag_core(q, i, {a2: wrap(me[a2] + 1), a3: far})

    def ag8(q):
        for i, a1, a2, a3 in parts_of(q):
            far = wrap(me[a3] + 2)
            ag_wait(q, i, 8, one_line)
            ag_core(q, i, {a2: wrap(me[a2] + 2), a3: far})

    def ag_core_wait(q):
        wait(g.at[1 - c, :, :, :, :, pl.ds(q * WIDTH, WIDTH)], dd_recv.at[q])

    def logits(m, core, first, last):
        def step(i, carry):
            rows = g[core, i, :, :, :, m * WIDTH:(m + 1) * WIDTH].reshape(T, WIDTH)
            weights, acc = (w, lg) if m == 0 else (wr, rlg)
            acc[...] += lax.dot_general(
                weights[i * 2 + core].reshape(VW, WIDTH), rows, (((1,), (1,)), ((), ())), preferred_element_type=f32
            )
            return carry

        lax.fori_loop(first, last, step, 0)

    def clear():
        lg[...] = jnp.zeros((VW, T), f32)
        rlg[...] = jnp.zeros((VW, T), f32)

    def local_stats():
        l, rf = lg[...], rlg[...]
        m = jnp.max(l, axis=0, keepdims=True)
        rm = jnp.max(rf, axis=0, keepdims=True)
        lm, rfm = l - m, rf - rm
        e = jnp.exp(lm)
        mass = jnp.sum(e, axis=0, keepdims=True)
        rmass = jnp.sum(jnp.exp(rfm), axis=0, keepdims=True)
        d = jnp.sum(e * (lm - rfm), axis=0, keepdims=True)
        st_s[0] = jnp.concatenate([m, mass, rm, rmass, d, d, d, d], axis=0)

    def stats_send(phase):
        for i, peer in enumerate(groups[phase]):
            send(
                st_s.at[phase], st_r.at[starts[phase] + i],
                st_send.at[phase], st_recv.at[phase], device(**peer),
            )

    def stats_wait(phase):
        n = len(groups[phase])
        wait(st_r.at[pl.ds(starts[phase], n)], st_recv.at[phase])
        terms = [st_s[phase]] + [st_r[starts[phase] + i] for i in range(n)]
        m = functools.reduce(jnp.maximum, [a[0:1] for a in terms])
        rm = functools.reduce(jnp.maximum, [a[2:3] for a in terms])
        mass, rmass, d = 0.0, 0.0, 0.0
        for a in terms:
            dm, drm = a[0:1] - m, a[2:3] - rm
            scale = jnp.exp(dm)
            mass += scale * a[1:2]
            rmass += jnp.exp(drm) * a[3:4]
            d += scale * (a[4:5] + a[1:2] * (dm - drm))
        st_s[phase + 1] = jnp.concatenate([m, mass, rm, rmass, d, d, d, d], axis=0)

    def grads():
        a = st_s[2]
        m, mass, rm, rmass, d = a[0:1], a[1:2], a[2:3], a[3:4], a[4:5]
        ln, rln = jnp.log(mass), jnp.log(rmass)
        divergence = d / mass - ln + rln
        weight = loss_scale * mask_ref[...].astype(f32)
        adv = adv_ref[...]
        place = ids_ref[...] - offset

        def step(i, carry):
            rows = pl.multiple_of(i * 128, 128)
            lp = (lg[pl.ds(rows, 128), :] - m) - ln
            rlp = (rlg[pl.ds(rows, 128), :] - rm) - rln
            p = jnp.exp(lp)
            entry = rows + lax.broadcasted_iota(jnp.int32, (128, T), 0)
            target = (entry == place).astype(f32)
            value = weight * (adv * (p - target) + penalty_weight * p * (lp - rlp - divergence))
            gv[pl.ds(rows, 128), :] = value.astype(bf16)
            gt[:, pl.ds(rows, 128)] = value.T.astype(bf16)
            return carry

        lax.fori_loop(0, VW // 128, step, 0)

    HALF = WIDTH // 2

    turns = (wrap(x + 2), wrap(x + 1), wrap(x - 1), x)

    def products_other(k):
        i = turns[k]
        for n in range(2):
            cols = slice(n * HALF, (n + 1) * HALF)
            rows = jnp.dot(gt[...], w[i * 2 + 1 - c, :, cols], preferred_element_type=f32)
            wr[i, :, :, :, cols] = rows.astype(bf16).reshape(4, 4, R, HALF)
        send(wr.at[i], g.at[c, i, :, :, :, pl.ds(WIDTH, WIDTH)], y_send, y_recv.at[k], device(dc=1))

    def products_own(k):
        i = turns[k]
        wait(g.at[1 - c, i, :, :, :, pl.ds(WIDTH, WIDTH)], y_recv.at[k])
        for n in range(2):
            cols = slice(n * HALF, (n + 1) * HALF)
            rows = jnp.dot(gt[...], w[i * 2 + c, :, cols], preferred_element_type=f32)
            theirs = g[1 - c, i, :, :, :, WIDTH + n * HALF:WIDTH + (n + 1) * HALF]
            rows += theirs.reshape(T, HALF).astype(f32)
            wr[4 + i, :, :, :, cols] = rows.astype(bf16).reshape(4, 4, R, HALF)

    def order(r):
        a1, a2, a3 = ORDERS[r]
        plane = tuple(a for a in (X, Y, Z) if a != a3)
        at = lambda ref, where: pick(ref, (), plane, where, REDUCE[r])
        line = lambda ref, where: pick(ref, (), (a1,), where, REDUCE[r])

        def mine(where):
            where = dict(where)
            j = where.get(X, ALL)
            where[X] = j + 4 if not isinstance(j, slice) else slice(4 + (j.start or 0), 4 + (j.stop or 4))
            return pick(wr, (), (X, Y, Z), where, REDUCE[r])

        return a1, a2, a3, at, line, mine

    def add(place, other):
        place[...] = (place[...].astype(f32) + other[...].astype(f32)).astype(bf16)

    def rs3_start(k):
        i, ss = turns[k], rs_send.at[0]
        a1, a2, a3, at, line, mine = order(0)
        right, left, far = wrap(z + 1), wrap(z - 1), wrap(z + 2)
        if k % 2 == 0:
            send(mine({X: i, Z: far}), at(fw, {X: i}), ss, rs3.at[0, 0, k], along(Z, 1))
            send(mine({X: i, Z: left}), at(rr, {X: i}), ss, rs3.at[0, 1, 0], along(Z, 3))
        else:
            send(mine({X: i, Z: far}), at(fw, {X: i}), ss, rs3.at[0, 0, k], along(Z, 3))
            send(mine({X: i, Z: right}), at(rl, {X: i}), ss, rs3.at[0, 1, 0], along(Z, 1))
        a1, a2, a3, at, line, mine = order(2)
        right, left, far = wrap(y + 1), wrap(y - 1), wrap(y + 2)
        send(mine({X: i, Y: far, Z: LOW}), at(fw, {X: i, Z: LOW}), ss, rs3.at[2, 0, k], along(Y, 1))
        send(mine({X: i, Y: far, Z: HIGH}), at(fw, {X: i, Z: HIGH}), ss, rs3.at[2, 0, k], along(Y, 3))
        send(mine({X: i, Y: right, Z: HIGH}), at(rl, {X: i, Z: HIGH}), ss, rs3.at[2, 1, k], along(Y, 1))
        send(mine({X: i, Y: left, Z: LOW}), at(rr, {X: i, Z: LOW}), ss, rs3.at[2, 1, k], along(Y, 3))
        a1, a2, a3, at, line, mine = order(1)
        if k == 0:
            send(mine({X: i, Y: LOW}), at(fw, {Y: LOW}), ss, rs3.at[1, 0, 0], along(X, 1))
            send(mine({X: i, Y: HIGH}), at(fw, {Y: HIGH}), ss, rs3.at[1, 0, 0], along(X, 3))
        elif k == 1:
            send(mine({X: i, Y: HIGH}), at(rl, {Y: HIGH}), ss, rs3.at[1, 1, 0], along(X, 1))
        elif k == 2:
            send(mine({X: i, Y: LOW}), at(rr, {Y: LOW}), ss, rs3.at[1, 1, 0], along(X, 3))

    def rs3_middle(k):
        i, ss = turns[k], rs_send.at[0]
        a1, a2, a3, at, line, mine = order(0)
        place = at(fw, {X: i})
        wait(place, rs3.at[0, 0, k])
        to, step, dst = (wrap(z + 1), 1, rl) if k % 2 == 0 else (wrap(z - 1), 3, rr)
        add(place, mine({X: i, Z: to}))
        send(place, at(dst, {X: i}), ss, rs3.at[0, 2, 0], along(Z, step))
        a1, a2, a3, at, line, mine = order(2)
        wait(at(fw, {X: i}), rs3.at[2, 0, k])
        for part, to, step, dst in ((LOW, wrap(y + 1), 1, rl), (HIGH, wrap(y - 1), 3, rr)):
            place = at(fw, {X: i, Z: part})
            add(place, mine({X: i, Y: to, Z: part}))
            send(place, at(dst, {X: i, Z: part}), ss, rs3.at[2, 2, k], along(Y, step))

    def rs3_middle_x():
        a1, a2, a3, at, line, mine = order(1)
        wait(at(fw, {}), rs3.at[1, 0, 0])
        for part, to, step, dst in ((LOW, turns[1], 1, rl), (HIGH, turns[2], 3, rr)):
            place = at(fw, {Y: part})
            add(place, mine({X: to, Y: part}))
            send(place, at(dst, {Y: part}), rs_send.at[0], rs3.at[1, 2, 0], along(X, step))

    def summed(at, where, own):
        total = own[...].astype(f32) + at(rl, where)[...].astype(f32) + at(rr, where)[...].astype(f32)
        at(t3, where)[...] = total.astype(bf16)

    def rs3_end_lines(k):
        i, ss = turns[k], rs_send.at[1]
        a1, a2, a3, at, line, mine = order(2)
        wait(at(rl, {X: i}), rs3.at[2, 1, k])
        wait(at(rr, {X: i}), rs3.at[2, 2, k])
        summed(at, {X: i}, mine({X: i, Y: y}))
        if k == 0:
            send(at(t3, {X: i, Z: LOW}), line(fw2, {Z: LOW}), ss, rs2.at[2, 0], along(X, 1))
            send(at(t3, {X: i, Z: HIGH}), line(fw2, {Z: HIGH}), ss, rs2.at[2, 0], along(X, 3))
        elif k == 1:
            send(at(t3, {X: i, Z: HIGH}), line(rl2, {Z: HIGH}), ss, rs2.at[2, 1], along(X, 1))
        elif k == 2:
            send(at(t3, {X: i, Z: LOW}), line(rr2, {Z: LOW}), ss, rs2.at[2, 1], along(X, 3))

    def rs3_end(r):
        ss = rs_send.at[1]
        a1, a2, a3, at, line, mine = order(r)
        wait(at(rl, {}), rs3.at[r, 1, 0])
        wait(at(rr, {}), rs3.at[r, 2, 0])
        summed(at, {}, mine({a3: me[a3]}))
        far, right, left = wrap(me[a2] + 2), wrap(me[a2] + 1), wrap(me[a2] - 1)
        send(at(t3, {a1: LOW, a2: far}), line(fw2, {a1: LOW}), ss, rs2.at[r, 0], along(a2, 1))
        send(at(t3, {a1: HIGH, a2: far}), line(fw2, {a1: HIGH}), ss, rs2.at[r, 0], along(a2, 3))
        send(at(t3, {a1: HIGH, a2: right}), line(rl2, {a1: HIGH}), ss, rs2.at[r, 1], along(a2, 1))
        send(at(t3, {a1: LOW, a2: left}), line(rr2, {a1: LOW}), ss, rs2.at[r, 1], along(a2, 3))

    def rs2_middle(r):
        a1, a2, a3, at, line, mine = order(r)
        wait(line(fw2, {}), rs2.at[r, 0])
        for part, to, step, dst in ((LOW, wrap(me[a2] + 1), 1, rl2), (HIGH, wrap(me[a2] - 1), 3, rr2)):
            place = line(fw2, {a1: part})
            add(place, at(t3, {a1: part, a2: to}))
            send(place, line(dst, {a1: part}), rs_send.at[1], rs2.at[r, 2], along(a2, step))

    def rs2_end(r):
        a1, a2, a3, at, line, mine = order(r)
        wait(line(rl2, {}), rs2.at[r, 1])
        wait(line(rr2, {}), rs2.at[r, 2])
        total = at(t3, {a2: me[a2]})[...].astype(f32) + line(rl2, {})[...].astype(f32)
        line(t2, {})[...] = total + line(rr2, {})[...].astype(f32)
        for k in (1, 2, 3):
            send(
                line(t2, {a1: wrap(me[a1] + k)}), line(r1, {a1: k - 1}), rs_send.at[2], rs1.at[r], along(a1, k)
            )

    def rs1_end(r):
        a1, a2, a3, at, line, mine = order(r)
        _, row, rows, col, cols = REDUCE[r]
        wait(line(r1, {}), rs1.at[r])
        total = line(t2, {a1: me[a1]})[...]
        for k in range(3):
            total += line(r1, {a1: k})[...]
        out_h[row:row + rows, col:col + cols] = total

    def head(first, last):
        def step(i, carry):
            rows = g[lax.rem(i, 2), i // 2, :, :, :, 0:WIDTH].reshape(T, WIDTH)
            total = jnp.dot(gv[...], rows, preferred_element_type=f32)
            out_w[:, pl.ds(pl.multiple_of(i * WIDTH, WIDTH), WIDTH)] = total.astype(bf16)
            return carry

        lax.fori_loop(first, last, step, 0)

    def weights_wait(m):
        ref = (w, wr)[m]
        wait(ref, load_sem.at[2 + m])

    def drain():
        wait(out_w.at[:, pl.ds(0, 63 * 128)], ag_send)
        wait(g.at[c], dd_send)
        for phase in range(2):
            n = len(groups[phase])
            wait(st_r.at[pl.ds(starts[phase], n)], st_send.at[phase])
        wait(wr.at[pl.ds(0, 4)], y_send)
        wait(wr.at[pl.ds(0, 3)], rs_send.at[0])
        wait(wr.at[0, pl.ds(0, 3)], rs_send.at[1])
        wait(t2.at[pl.ds(0, 3)], rs_send.at[2])

    ag0(0)
    ag0(1)
    weights_start()
    clear()
    for step in (ag1, ag2, ag3, ag4, ag5, ag6, ag7, ag8):
        step(0)
        step(1)
    weights_wait(0)
    logits(0, c, 0, 4)
    weights_wait(1)
    logits(1, c, 0, 4)
    ag_core_wait(0)
    logits(0, 1 - c, 0, 4)
    ag_core_wait(1)
    logits(1, 1 - c, 0, 4)
    local_stats()
    stats_send(0)
    stats_wait(0)
    stats_send(1)
    stats_wait(1)
    grads()
    products_other(0)
    products_other(1)
    products_own(0)
    rs3_start(0)
    products_other(2)
    products_own(1)
    rs3_start(1)
    products_other(3)
    products_own(2)
    rs3_start(2)
    rs3_middle(0)
    products_own(3)
    rs3_start(3)
    rs3_middle(1)
    rs3_middle_x()
    head(0, 1)
    rs3_middle(2)
    head(1, 2)
    rs3_middle(3)
    head(2, 4)
    rs3_end_lines(0)
    rs3_end_lines(1)
    head(4, 5)
    rs3_end_lines(2)
    rs3_end(1)
    head(5, 6)
    rs2_middle(2)
    rs3_end_lines(3)
    rs3_end(0)
    rs2_middle(1)
    rs2_end(2)
    head(6, 7)
    rs2_middle(0)
    rs2_end(1)
    rs2_end(0)
    head(7, 8)
    rs1_end(2)
    rs1_end(1)
    rs1_end(0)
    drain()


def shards(hidden, ref_hidden, w_policy, w_ref, token_ids, loss_mask, advantages):
    any_space = pl.BlockSpec(memory_space=pl.ANY)
    vmem = pl.BlockSpec(memory_space=pltpu.VMEM)
    dma = pltpu.SemaphoreType.DMA
    return pl.pallas_call(
        kernel,
        out_shape=(
            pltpu.VMEM((R, WIDTH), f32),
            pltpu.VMEM((VW, 8 * WIDTH), bf16),
        ),
        in_specs=[any_space] * 4 + [vmem] * 3,
        out_specs=(vmem, vmem),
        scratch_shapes=[
            pltpu.VMEM((2, 4, 4, 4, R, 2 * WIDTH), bf16),
            pltpu.VMEM((8, VW, WIDTH), bf16),
            pltpu.VMEM((8, 4, 4, R, WIDTH), bf16),
            pltpu.VMEM((VW, T), f32),
            pltpu.VMEM((VW, T), f32),
            pltpu.VMEM((VW, T), bf16),
            pltpu.VMEM((T, VW), bf16),
            pltpu.VMEM((3, 8, T), f32),
            pltpu.VMEM((22, 8, T), f32),
            pltpu.VMEM((4, 4, R, WIDTH), bf16),
            pltpu.VMEM((4, 4, R, WIDTH), bf16),
            pltpu.VMEM((4, 4, R, WIDTH), bf16),
            pltpu.VMEM((4, 4, R, WIDTH), bf16),
            pltpu.VMEM((4, R, WIDTH), bf16),
            pltpu.VMEM((4, R, WIDTH), bf16),
            pltpu.VMEM((4, R, WIDTH), bf16),
            pltpu.VMEM((4, R, WIDTH), f32),
            pltpu.VMEM((3, R, WIDTH), f32),
            dma((4,)),
            dma,
            dma((ROUNDS, PARTS, 9)),
            dma,
            dma((ROUNDS,)),
            dma((2,)),
            dma((2,)),
            dma,
            dma((4,)),
            dma((3,)),
            dma((3, 3, 4)),
            dma((3, 3)),
            dma((3,)),
        ],
        compiler_params=pltpu.CompilerParams(
            collective_id=0, has_side_effects=True, vmem_limit_bytes=46 * 2**20
        ),
        cost_estimate=pl.CostEstimate(flops=4 * 2 * 512 * 512 * 8192, bytes_accessed=3 * 2**23, transcendentals=2**20),
        name="head_step",
    )(
        hidden, ref_hidden, w_policy, w_ref.reshape(4, 4, R, 8 * WIDTH),
        token_ids.reshape(1, T), loss_mask.reshape(1, T), advantages.reshape(1, T),
    )


def solution(mesh):
    placed = (
        P("section", "tensor"),
        P("section", "tensor"),
        P(("section", "tensor"), None),
        P(("section", "tensor"), None),
        P(),
        P(),
        P(),
    )
    return jax.shard_map(
        shards,
        mesh=mesh,
        in_specs=placed,
        out_specs=(P("section", "tensor"), P(("section", "tensor"), None)),
        check_vma=False,
    )
```

time: 530 us -> 104 us (0.20)
  waiting for transfers between devices: 253 us -> 0 us
  blocking collectives: 221 us -> 0 us
  Pallas kernels: 0 us -> 99.1 us
  matrix products: 40.8 us -> 0 us
  between operations: 13.8 us -> 0.64 us
    reduce_scatter x2 -> x0, waiting for transfers between devices: 132 us -> none  [the longest x1 108 us: shards(): lax.psum_scatter(jnp.dot(grad_logits, w_policy, preferred_element_type=jn...]
    psum x2 -> x0, blocking collectives: 127 us -> none  [the longest x1 64.3 us: shards(): lax.psum((jnp.sum(jnp.exp(logits - maximum[:, None]), axis=1), jnp.sum(jn...]
    all_gather x2 -> x0, waiting for transfers between devices: 121 us -> none  [the longest x1 63.1 us: shards(): full_hidden = lax.all_gather(features, 'section', axis=0, tiled=True)]
    pallas_call x0 -> x1, Pallas kernels: none -> 99.1 us  [shards(): pl.pallas_call(kernel, out_shape=(pltpu.VMEM((R, WIDTH), f32), pltpu.VMEM...]
    pmax x1 -> x0, blocking collectives: 64.5 us -> none  [shards(): lax.pmax((jnp.max(logits, axis=1), jnp.max(ref_logits, axis=1)), ('sectio...]
    dot_general x4 -> x0, matrix products: 40.8 us -> none  [the longest x1 11.5 us: shards(): jnp.dot(grad_logits, w_policy, preferred_element_type=jnp.float32)]
    all_gather x2 -> x0, blocking collectives: 29.3 us -> none  [the longest x1 14.9 us: shards(): lax.all_gather(ref_hidden, 'tensor', axis=1, tiled=True)]
  transfers between devices with their start and end apart: 4 -> 0, of which waited for: 4 -> 0; matrix products, arithmetic and copies ran while one was open for 4% -> 0% of each run, Pallas kernels for 0% -> 0%
where the time goes in v2:
time: 104 us
  Pallas kernels  99.1 us (95%)
  local copies, waits for them, and re-layouts  4.05 us (4%)
    pallas_call x1, Pallas kernels, shards(): pl.pallas_call(kernel, out_shape=(pltpu.VMEM((R, WIDTH), f32), pltpu.VMEM...  99.1 us
    unnamed x2, local copies, waits for them, and re-layouts  4.05 us

profile of v2, /device:TPU:0, one launch (start us, length us, event | category | flops | bytes accessed | tf_op | source)
XLA Modules:
  0.0 103.8 jit_solution(2968756138995743879)
XLA Ops:
  0.6 99.1 %head_step.1 = (f32[32,1024]{1,0:T(8,128)S(1)}, bf16[512,8192]{1,0:T(8,128)(2,1)S(1)}) custom-call(bf16[32,1024]{1,0:T(8,128)(2,1)} %hid.1, bf16[32,1024]{1,0:T(8,128)(2,1)} %rhid.1, bf16[512,8192]{1,0:T(8,128)(2,1)} %w_hbm.1, bf16[4,4,32,8192]{3,2,1,0:T(8,128)(2,1)} %bitcast.4, s32[1,512]{1,0:T(1,128)} %bitcast.5, s32[1,512]{1,0:T(1,128)} %bitcast.6, ...), custom_call_target="tpu_custom_call" | custom-call | flops 17179869184 | bytes 25165824 | tf_op jit(solution)/shard_map/head_step/pallas_call | solution.py:508
  99.7 0.7 copy.11
  100.4 3.4 %copy.12 = bf16[512,8192]{1,0:T(8,128)(2,1)} copy(bf16[512,8192]{1,0:T(8,128)(2,1)S(1)} %get-tuple-element.3) | data formatting | bytes 16777216

commit v3 on v2

--- a/solution.py
+++ b/solution.py
@@ -19,11 +19,13 @@
 VW = 512
 X, Y, Z = 0, 1, 2
 ORDERS = ((X, Y, Z), (Y, Z, X), (Z, X, Y))
+SUM_ORDERS = ((Y, X, Z), (Z, Y, X), (Z, X, Y))
 GATHER = (
-    ((0, 0, 32, 0, 384), (1, 0, 32, 384, 384), (2, 0, 32, 768, 256)),
-    ((0, 0, 32, 1024, 256), (1, 0, 32, 1280, 256), (2, 0, 32, 1536, 384), (0, 0, 16, 1920, 128), (1, 16, 16, 1920, 128)),
+    ((0, 0, 32, 0, 384), (2, 0, 32, 384, 384), (1, 0, 32, 768, 256)),
+    ((0, 0, 32, 1024, 256), (2, 0, 32, 1280, 256), (0, 0, 16, 1536, 128), (2, 16, 16, 1536, 128), (1, 0, 32, 1664, 384)),
 )
-REDUCE = ((0, 0, 32, 0, 256), (1, 0, 32, 256, 384), (2, 0, 32, 640, 384))
+EARLY = (768, 640)
+REDUCE = ((0, 0, 32, 0, 384), (1, 0, 32, 384, 256), (2, 0, 32, 640, 384))
 ROUNDS, PARTS = 2, 5
 ALL = slice(None)
 LOW, HIGH = slice(0, 2), slice(2, 4)
@@ -31,6 +33,14 @@
 
 def wrap(i):
     return lax.rem(i + 4, 4)
+
+
+def two_rows(a):
+    return jnp.concatenate([a[:, :T // 2], a[:, T // 2:]], axis=0)
+
+
+def one_row(a):
+    return jnp.concatenate([a[0:1], a[1:2]], axis=1)
 
 
 def pick(ref, lead, axes, where, part):
@@ -108,9 +118,9 @@
         part = ag_part(GATHER[q][i], where)
         send(part, part, ag_send, ag_recv.at[q, i, event], along(axis, k))
 
-    def ag_core(q, i, where):
+    def ag_core(q, i, where, plane):
         part = ag_part(GATHER[q][i], where)
-        send(part, part, dd_send, dd_recv.at[q], device(dc=1))
+        send(part, part, dd_send, dd_recv.at[q, i, plane], device(dc=1))
 
     def ag_wait(q, i, event, where):
         wait(ag_part(GATHER[q][i], where), ag_recv.at[q, i, event])
@@ -157,8 +167,8 @@
             ag_send_part(q, i, {a1: LOW, a2: j, a3: left}, a3, 1, event + 3)
             ag_send_part(q, i, {a1: HIGH, a2: j, a3: right}, a3, 3, event + 3)
         for j in lines:
-            ag_core(q, i, {a2: j, a3: left})
-            ag_core(q, i, {a2: j, a3: right})
+            ag_core(q, i, {a2: j, a3: left}, 1)
+            ag_core(q, i, {a2: j, a3: right}, 1)
 
     def ag3(q):
         for i, a1, a2, a3 in parts_of(q):
@@ -170,7 +180,7 @@
             line = {a2: wrap(me[a2] + 2), a3: me[a3]}
             for k in (1, 3):
                 ag_send_part(q, i, line, a3, k, 5)
-            ag_core(q, i, {a3: me[a3]})
+            ag_core(q, i, {a3: me[a3]}, 0)
 
     def ag5(q):
         for i, a1, a2, a3 in parts_of(q):
@@ -184,30 +194,53 @@
         for i, a1, a2, a3 in parts_of(q):
             far = wrap(me[a3] + 2)
             ag_wait(q, i, 6, one_line)
-            ag_core(q, i, {a2: me[a2], a3: far})
+            ag_core(q, i, {a2: me[a2], a3: far}, 2)
             ag_wait(q, i, 7, two_lines)
-            ag_core(q, i, {a2: wrap(me[a2] - 1), a3: far})
-            ag_core(q, i, {a2: wrap(me[a2] + 1), a3: far})
+            ag_core(q, i, {a2: wrap(me[a2] - 1), a3: far}, 2)
+            ag_core(q, i, {a2: wrap(me[a2] + 1), a3: far}, 2)
 
     def ag8(q):
         for i, a1, a2, a3 in parts_of(q):
             far = wrap(me[a3] + 2)
             ag_wait(q, i, 8, one_line)
-            ag_core(q, i, {a2: wrap(me[a2] + 2), a3: far})
-
-    def ag_core_wait(q):
-        wait(g.at[1 - c, :, :, :, :, pl.ds(q * WIDTH, WIDTH)], dd_recv.at[q])
-
-    def logits(m, core, first, last):
-        def step(i, carry):
-            rows = g[core, i, :, :, :, m * WIDTH:(m + 1) * WIDTH].reshape(T, WIDTH)
-            weights, acc = (w, lg) if m == 0 else (wr, rlg)
-            acc[...] += lax.dot_general(
-                weights[i * 2 + core].reshape(VW, WIDTH), rows, (((1,), (1,)), ((), ())), preferred_element_type=f32
-            )
+            ag_core(q, i, {a2: wrap(me[a2] + 2), a3: far}, 2)
+
+    def ag_core_wait(q, i, plane):
+        planes = pl.ds(0, 2) if plane == 1 else 0
+        wait(pick(g, (1 - c,), (X, Y, Z), {X: planes}, GATHER[q][i]), dd_recv.at[q, i, plane])
+
+    def early_core_wait(plane):
+        for q in range(ROUNDS):
+            ag_core_wait(q, len(GATHER[q]) - 1, plane)
+
+    def late_core_wait():
+        for q in range(ROUNDS):
+            for i in range(len(GATHER[q]) - 1):
+                for plane in range(3):
+                    ag_core_wait(q, i, plane)
+
+    def logits(m, core, chips, first, last):
+        rows = [g[core, i, :, :, :, m * WIDTH + first:m * WIDTH + last].reshape(T, last - first) for i in chips]
+        if m == 0:
+            weights = [w[i * 2 + core, :, first:last] for i in chips]
+        else:
+            weights = [wr[i * 2 + core, :, :, :, first:last].reshape(VW, last - first) for i in chips]
+        acc = (lg, rlg)[m]
+        acc[...] += lax.dot_general(
+            jnp.concatenate(weights, axis=1), jnp.concatenate(rows, axis=1),
+            (((1,), (1,)), ((), ())), preferred_element_type=f32,
+        )
+
+    def early_logits(core, first, count, stride=1):
+        def step(j, carry):
+            for m in range(2):
+                logits(m, core, (wrap(x + first + stride * j),), EARLY[m], WIDTH)
             return carry
 
-        lax.fori_loop(first, last, step, 0)
+        lax.fori_loop(0, count, step, 0)
+
+    def late_logits(m, core):
+        logits(m, core, (0, 1, 2, 3), 0, EARLY[m])
 
     def clear():
         lg[...] = jnp.zeros((VW, T), f32)
@@ -222,7 +255,9 @@
         mass = jnp.sum(e, axis=0, keepdims=True)
         rmass = jnp.sum(jnp.exp(rfm), axis=0, keepdims=True)
         d = jnp.sum(e * (lm - rfm), axis=0, keepdims=True)
-        st_s[0] = jnp.concatenate([m, mass, rm, rmass, d, d, d, d], axis=0)
+        ln, rln = jnp.log(mass), jnp.log(rmass)
+        lse, rlse, kl = two_rows(m + ln), two_rows(rm + rln), two_rows(d / mass - ln + rln)
+        st_s[0] = jnp.concatenate([lse, rlse, kl, kl], axis=0)
 
     def stats_send(phase):
         for i, peer in enumerate(groups[phase]):
@@ -235,30 +270,26 @@
         n = len(groups[phase])
         wait(st_r.at[pl.ds(starts[phase], n)], st_recv.at[phase])
         terms = [st_s[phase]] + [st_r[starts[phase] + i] for i in range(n)]
-        m = functools.reduce(jnp.maximum, [a[0:1] for a in terms])
-        rm = functools.reduce(jnp.maximum, [a[2:3] for a in terms])
-        mass, rmass, d = 0.0, 0.0, 0.0
-        for a in terms:
-            dm, drm = a[0:1] - m, a[2:3] - rm
-            scale = jnp.exp(dm)
-            mass += scale * a[1:2]
-            rmass += jnp.exp(drm) * a[3:4]
-            d += scale * (a[4:5] + a[1:2] * (dm - drm))
-        st_s[phase + 1] = jnp.concatenate([m, mass, rm, rmass, d, d, d, d], axis=0)
+        m = functools.reduce(jnp.maximum, [a[0:2] for a in terms])
+        rm = functools.reduce(jnp.maximum, [a[2:4] for a in terms])
+        shares = [jnp.exp(a[0:2] - m) for a in terms]
+        mass = sum(shares)
+        lse = m + jnp.log(mass)
+        rlse = rm + jnp.log(sum(jnp.exp(a[2:4] - rm) for a in terms))
+        kl = sum(e * (a[4:6] + (a[0:2] - lse) - (a[2:4] - rlse)) for e, a in zip(shares, terms)) / mass
+        st_s[phase + 1] = jnp.concatenate([lse, rlse, kl, kl], axis=0)
 
     def grads():
         a = st_s[2]
-        m, mass, rm, rmass, d = a[0:1], a[1:2], a[2:3], a[3:4], a[4:5]
-        ln, rln = jnp.log(mass), jnp.log(rmass)
-        divergence = d / mass - ln + rln
+        lse, rlse, divergence = one_row(a[0:2]), one_row(a[2:4]), one_row(a[4:6])
         weight = loss_scale * mask_ref[...].astype(f32)
         adv = adv_ref[...]
         place = ids_ref[...] - offset
 
         def step(i, carry):
             rows = pl.multiple_of(i * 128, 128)
-            lp = (lg[pl.ds(rows, 128), :] - m) - ln
-            rlp = (rlg[pl.ds(rows, 128), :] - rm) - rln
+            lp = lg[pl.ds(rows, 128), :] - lse
+            rlp = rlg[pl.ds(rows, 128), :] - rlse
             p = jnp.exp(lp)
             entry = rows + lax.broadcasted_iota(jnp.int32, (128, T), 0)
             target = (entry == place).astype(f32)
@@ -269,30 +300,23 @@
 
         lax.fori_loop(0, VW // 128, step, 0)
 
-    HALF = WIDTH // 2
-
     turns = (wrap(x + 2), wrap(x + 1), wrap(x - 1), x)
 
     def products_other(k):
         i = turns[k]
-        for n in range(2):
-            cols = slice(n * HALF, (n + 1) * HALF)
-            rows = jnp.dot(gt[...], w[i * 2 + 1 - c, :, cols], preferred_element_type=f32)
-            wr[i, :, :, :, cols] = rows.astype(bf16).reshape(4, 4, R, HALF)
+        rows = jnp.dot(gt[...], w[i * 2 + 1 - c], preferred_element_type=f32)
+        wr[i] = rows.astype(bf16).reshape(4, 4, R, WIDTH)
         send(wr.at[i], g.at[c, i, :, :, :, pl.ds(WIDTH, WIDTH)], y_send, y_recv.at[k], device(dc=1))
 
     def products_own(k):
         i = turns[k]
+        rows = jnp.dot(gt[...], w[i * 2 + c], preferred_element_type=f32)
         wait(g.at[1 - c, i, :, :, :, pl.ds(WIDTH, WIDTH)], y_recv.at[k])
-        for n in range(2):
-            cols = slice(n * HALF, (n + 1) * HALF)
-            rows = jnp.dot(gt[...], w[i * 2 + c, :, cols], preferred_element_type=f32)
-            theirs = g[1 - c, i, :, :, :, WIDTH + n * HALF:WIDTH + (n + 1) * HALF]
-            rows += theirs.reshape(T, HALF).astype(f32)
-            wr[4 + i, :, :, :, cols] = rows.astype(bf16).reshape(4, 4, R, HALF)
+        rows += g[1 - c, i, :, :, :, WIDTH:2 * WIDTH].reshape(T, WIDTH).astype(f32)
+        wr[4 + i] = rows.astype(bf16).reshape(4, 4, R, WIDTH)
 
     def order(r):
-        a1, a2, a3 = ORDERS[r]
+        a1, a2, a3 = SUM_ORDERS[r]
         plane = tuple(a for a in (X, Y, Z) if a != a3)
         at = lambda ref, where: pick(ref, (), plane, where, REDUCE[r])
         line = lambda ref, where: pick(ref, (), (a1,), where, REDUCE[r])
@@ -310,51 +334,49 @@
 
     def rs3_start(k):
         i, ss = turns[k], rs_send.at[0]
-        a1, a2, a3, at, line, mine = order(0)
-        right, left, far = wrap(z + 1), wrap(z - 1), wrap(z + 2)
-        if k % 2 == 0:
-            send(mine({X: i, Z: far}), at(fw, {X: i}), ss, rs3.at[0, 0, k], along(Z, 1))
-            send(mine({X: i, Z: left}), at(rr, {X: i}), ss, rs3.at[0, 1, 0], along(Z, 3))
-        else:
-            send(mine({X: i, Z: far}), at(fw, {X: i}), ss, rs3.at[0, 0, k], along(Z, 3))
-            send(mine({X: i, Z: right}), at(rl, {X: i}), ss, rs3.at[0, 1, 0], along(Z, 1))
-        a1, a2, a3, at, line, mine = order(2)
-        right, left, far = wrap(y + 1), wrap(y - 1), wrap(y + 2)
-        send(mine({X: i, Y: far, Z: LOW}), at(fw, {X: i, Z: LOW}), ss, rs3.at[2, 0, k], along(Y, 1))
-        send(mine({X: i, Y: far, Z: HIGH}), at(fw, {X: i, Z: HIGH}), ss, rs3.at[2, 0, k], along(Y, 3))
-        send(mine({X: i, Y: right, Z: HIGH}), at(rl, {X: i, Z: HIGH}), ss, rs3.at[2, 1, k], along(Y, 1))
-        send(mine({X: i, Y: left, Z: LOW}), at(rr, {X: i, Z: LOW}), ss, rs3.at[2, 1, k], along(Y, 3))
-        a1, a2, a3, at, line, mine = order(1)
+        for r in (0, 2):
+            a1, a2, a3, at, line, mine = order(r)
+            for part, step in ((LOW, 1), (HIGH, 3)):
+                send(
+                    mine({X: i, a3: wrap(me[a3] + 2), a1: part}), at(fw, {X: i, a1: part}),
+                    ss, rs3.at[r, 0, k], along(a3, step),
+                )
         if k == 0:
-            send(mine({X: i, Y: LOW}), at(fw, {Y: LOW}), ss, rs3.at[1, 0, 0], along(X, 1))
-            send(mine({X: i, Y: HIGH}), at(fw, {Y: HIGH}), ss, rs3.at[1, 0, 0], along(X, 3))
-        elif k == 1:
-            send(mine({X: i, Y: HIGH}), at(rl, {Y: HIGH}), ss, rs3.at[1, 1, 0], along(X, 1))
-        elif k == 2:
-            send(mine({X: i, Y: LOW}), at(rr, {Y: LOW}), ss, rs3.at[1, 1, 0], along(X, 3))
+            a1, a2, a3, at, line, mine = order(1)
+            for part, step in ((LOW, 1), (HIGH, 3)):
+                send(mine({X: i, a1: part}), at(fw, {a1: part}), ss, rs3.at[1, 0, 0], along(X, step))
+
+    def rs3_raw(k):
+        i, ss = turns[k], rs_send.at[0]
+        for r in (0, 2):
+            a1, a2, a3, at, line, mine = order(r)
+            for part, step, dst in ((HIGH, 1, rl), (LOW, 3, rr)):
+                send(
+                    mine({X: i, a3: wrap(me[a3] + step), a1: part}), at(dst, {X: i, a1: part}),
+                    ss, rs3.at[r, 1, k], along(a3, step),
+                )
+        if k in (1, 2):
+            a1, a2, a3, at, line, mine = order(1)
+            part, step, dst = ((HIGH, 1, rl), (LOW, 3, rr))[k - 1]
+            send(mine({X: i, a1: part}), at(dst, {a1: part}), ss, rs3.at[1, 1, 0], along(X, step))
 
     def rs3_middle(k):
         i, ss = turns[k], rs_send.at[0]
-        a1, a2, a3, at, line, mine = order(0)
-        place = at(fw, {X: i})
-        wait(place, rs3.at[0, 0, k])
-        to, step, dst = (wrap(z + 1), 1, rl) if k % 2 == 0 else (wrap(z - 1), 3, rr)
-        add(place, mine({X: i, Z: to}))
-        send(place, at(dst, {X: i}), ss, rs3.at[0, 2, 0], along(Z, step))
-        a1, a2, a3, at, line, mine = order(2)
-        wait(at(fw, {X: i}), rs3.at[2, 0, k])
-        for part, to, step, dst in ((LOW, wrap(y + 1), 1, rl), (HIGH, wrap(y - 1), 3, rr)):
-            place = at(fw, {X: i, Z: part})
-            add(place, mine({X: i, Y: to, Z: part}))
-            send(place, at(dst, {X: i, Z: part}), ss, rs3.at[2, 2, k], along(Y, step))
+        for r in (0, 2):
+            a1, a2, a3, at, line, mine = order(r)
+            wait(at(fw, {X: i}), rs3.at[r, 0, k])
+            for part, step, dst in ((LOW, 1, rl), (HIGH, 3, rr)):
+                place = at(fw, {X: i, a1: part})
+                add(place, mine({X: i, a3: wrap(me[a3] + step), a1: part}))
+                send(place, at(dst, {X: i, a1: part}), ss, rs3.at[r, 2, k], along(a3, step))
 
     def rs3_middle_x():
         a1, a2, a3, at, line, mine = order(1)
         wait(at(fw, {}), rs3.at[1, 0, 0])
         for part, to, step, dst in ((LOW, turns[1], 1, rl), (HIGH, turns[2], 3, rr)):
-            place = at(fw, {Y: part})
-            add(place, mine({X: to, Y: part}))
-            send(place, at(dst, {Y: part}), rs_send.at[0], rs3.at[1, 2, 0], along(X, step))
+            place = at(fw, {a1: part})
+            add(place, mine({X: to, a1: part}))
+            send(place, at(dst, {a1: part}), rs_send.at[0], rs3.at[1, 2, 0], along(X, step))
 
     def summed(at, where, own):
         total = own[...].astype(f32) + at(rl, where)[...].astype(f32) + at(rr, where)[...].astype(f32)
@@ -362,17 +384,18 @@
 
     def rs3_end_lines(k):
         i, ss = turns[k], rs_send.at[1]
-        a1, a2, a3, at, line, mine = order(2)
-        wait(at(rl, {X: i}), rs3.at[2, 1, k])
-        wait(at(rr, {X: i}), rs3.at[2, 2, k])
-        summed(at, {X: i}, mine({X: i, Y: y}))
-        if k == 0:
-            send(at(t3, {X: i, Z: LOW}), line(fw2, {Z: LOW}), ss, rs2.at[2, 0], along(X, 1))
-            send(at(t3, {X: i, Z: HIGH}), line(fw2, {Z: HIGH}), ss, rs2.at[2, 0], along(X, 3))
-        elif k == 1:
-            send(at(t3, {X: i, Z: HIGH}), line(rl2, {Z: HIGH}), ss, rs2.at[2, 1], along(X, 1))
-        elif k == 2:
-            send(at(t3, {X: i, Z: LOW}), line(rr2, {Z: LOW}), ss, rs2.at[2, 1], along(X, 3))
+        for r in (0, 2):
+            a1, a2, a3, at, line, mine = order(r)
+            wait(at(rl, {X: i}), rs3.at[r, 1, k])
+            wait(at(rr, {X: i}), rs3.at[r, 2, k])
+            summed(at, {X: i}, mine({X: i, a3: me[a3]}))
+            if k == 0:
+                send(at(t3, {X: i, a1: LOW}), line(fw2, {a1: LOW}), ss, rs2.at[r, 0], along(X, 1))
+                send(at(t3, {X: i, a1: HIGH}), line(fw2, {a1: HIGH}), ss, rs2.at[r, 0], along(X, 3))
+            elif k == 1:
+                send(at(t3, {X: i, a1: HIGH}), line(rl2, {a1: HIGH}), ss, rs2.at[r, 1], along(X, 1))
+            elif k == 2:
+                send(at(t3, {X: i, a1: LOW}), line(rr2, {a1: LOW}), ss, rs2.at[r, 1], along(X, 3))
 
     def rs3_end(r):
         ss = rs_send.at[1]
@@ -442,17 +465,33 @@
     ag0(1)
     weights_start()
     clear()
-    for step in (ag1, ag2, ag3, ag4, ag5, ag6, ag7, ag8):
+    for step in (ag1, ag2, ag3, ag4):
         step(0)
         step(1)
     weights_wait(0)
-    logits(0, c, 0, 4)
     weights_wait(1)
-    logits(1, c, 0, 4)
-    ag_core_wait(0)
-    logits(0, 1 - c, 0, 4)
-    ag_core_wait(1)
-    logits(1, 1 - c, 0, 4)
+    early_logits(c, 0, 1)
+    ag5(0)
+    ag5(1)
+    early_core_wait(0)
+    early_logits(1 - c, 0, 1)
+    ag6(0)
+    ag6(1)
+    early_logits(c, 1, 2, 2)
+    ag7(0)
+    ag7(1)
+    early_core_wait(1)
+    early_logits(1 - c, 1, 2, 2)
+    ag8(0)
+    ag8(1)
+    late_logits(0, c)
+    late_logits(1, c)
+    early_logits(c, 2, 1)
+    early_core_wait(2)
+    early_logits(1 - c, 2, 1)
+    late_core_wait()
+    late_logits(0, 1 - c)
+    late_logits(1, 1 - c)
     local_stats()
     stats_send(0)
     stats_wait(0)
@@ -466,38 +505,40 @@
     products_other(2)
     products_own(1)
     rs3_start(1)
+    rs3_raw(0)
     products_other(3)
     products_own(2)
     rs3_start(2)
     rs3_middle(0)
+    rs3_raw(1)
     products_own(3)
     rs3_start(3)
     rs3_middle(1)
+    rs3_raw(2)
     rs3_middle_x()
+    rs3_raw(3)
+    rs3_middle(2)
     head(0, 1)
-    rs3_middle(2)
+    rs3_middle(3)
     head(1, 2)
-    rs3_middle(3)
-    head(2, 4)
     rs3_end_lines(0)
+    head(2, 3)
     rs3_end_lines(1)
-    head(4, 5)
+    rs3_end(1)
+    head(3, 4)
     rs3_end_lines(2)
-    rs3_end(1)
-    head(5, 6)
+    rs2_middle(0)
     rs2_middle(2)
+    rs2_middle(1)
+    head(4, 6)
     rs3_end_lines(3)
-    rs3_end(0)
-    rs2_middle(1)
-    rs2_end(2)
-    head(6, 7)
-    rs2_middle(0)
     rs2_end(1)
     rs2_end(0)
-    head(7, 8)
-    rs1_end(2)
+    rs2_end(2)
+    head(6, 8)
     rs1_end(1)
     rs1_end(0)
+    rs1_end(2)
     drain()
 
 
@@ -521,8 +562,8 @@
             pltpu.VMEM((VW, T), f32),
             pltpu.VMEM((VW, T), bf16),
             pltpu.VMEM((T, VW), bf16),
-            pltpu.VMEM((3, 8, T), f32),
-            pltpu.VMEM((22, 8, T), f32),
+            pltpu.VMEM((3, 8, T // 2), f32),
+            pltpu.VMEM((22, 8, T // 2), f32),
             pltpu.VMEM((4, 4, R, WIDTH), bf16),
             pltpu.VMEM((4, 4, R, WIDTH), bf16),
             pltpu.VMEM((4, 4, R, WIDTH), bf16),
@@ -536,7 +577,7 @@
             dma,
             dma((ROUNDS, PARTS, 9)),
             dma,
-            dma((ROUNDS,)),
+            dma((ROUNDS, PARTS, 3)),
             dma((2,)),
             dma((2,)),
             dma,

time: 104 us -> 94.8 us (0.912)
  Pallas kernels: 99.1 us -> 90 us
    pallas_call x1, Pallas kernels: 99.1 us -> 90 us  [shards(): pl.pallas_call(kernel, out_shape=(pltpu.VMEM((R, WIDTH), f32), pltpu.VMEM...]
where the time goes in v3:
time: 94.8 us; the launch traced here: 94.7 us
  Pallas kernels  90 us (95%)
  local copies, waits for them, and re-layouts  4.05 us (4%)
    pallas_call x1, Pallas kernels, shards(): pl.pallas_call(kernel, out_shape=(pltpu.VMEM((R, WIDTH), f32), pltpu.VMEM...  90 us
    unnamed x2, local copies, waits for them, and re-layouts  4.05 us

profile of v3, /device:TPU:0, one launch (start us, length us, event | category | flops | bytes accessed | tf_op | source)
XLA Modules:
  0.0 94.7 jit_solution(5813399759852923048)
XLA Ops:
  0.6 90.0 %head_step.1 = (f32[32,1024]{1,0:T(8,128)S(1)}, bf16[512,8192]{1,0:T(8,128)(2,1)S(1)}) custom-call(bf16[32,1024]{1,0:T(8,128)(2,1)} %hid.1, bf16[32,1024]{1,0:T(8,128)(2,1)} %rhid.1, bf16[512,8192]{1,0:T(8,128)(2,1)} %w_hbm.1, bf16[4,4,32,8192]{3,2,1,0:T(8,128)(2,1)} %bitcast.4, s32[1,512]{1,0:T(1,128)} %bitcast.5, s32[1,512]{1,0:T(1,128)} %bitcast.6, ...), custom_call_target="tpu_custom_call" | custom-call | flops 17179869184 | bytes 25165824 | tf_op jit(solution)/shard_map/head_step/pallas_call | solution.py:549
  90.6 0.7 copy.11
  91.3 3.4 %copy.12 = bf16[512,8192]{1,0:T(8,128)(2,1)} copy(bf16[512,8192]{1,0:T(8,128)(2,1)S(1)} %get-tuple-element.3) | data formatting | bytes 16777216

commit v4 on v3

--- a/solution.py
+++ b/solution.py
@@ -52,10 +52,10 @@
 
 def kernel(
     hid, rhid, w_hbm, wr_hbm, ids_ref, mask_ref, adv_ref, out_h, out_w,
-    g, w, wr, lg, rlg, gv, gt, st_s, st_r,
+    g, w, wr, w2, lg, rlg, gv, gt, st_s, st_r,
     fw, rl, rr, t3, fw2, rl2, rr2, t2, r1,
     load_sem, ag_send, ag_recv, dd_send, dd_recv, st_send, st_recv,
-    y_send, y_recv, rs_send, rs3, rs2, rs1,
+    swap_send, swap_recv, rs_send, rs3, rs2, rs1,
 ):
     section, tensor = lax.axis_index("section"), lax.axis_index("tensor")
     x, c = tensor // 2, lax.rem(tensor, 2)
@@ -110,6 +110,9 @@
         for i in range(8):
             cols = pl.ds(i * WIDTH, WIDTH)
             pltpu.make_async_copy(wr_hbm.at[:, :, :, cols], wr.at[i], load_sem.at[3]).start()
+        for i in range(4):
+            cols = pl.ds(pl.multiple_of((i * 2 + 1 - c) * WIDTH, WIDTH), WIDTH)
+            send(w_hbm.at[:, cols], w2.at[i], swap_send.at[0], swap_recv.at[0], device(dc=1))
 
     def ag_part(part, where):
         return pick(g, (c,), (X, Y, Z), where, part)
@@ -295,25 +298,25 @@
             target = (entry == place).astype(f32)
             value = weight * (adv * (p - target) + penalty_weight * p * (lp - rlp - divergence))
             gv[pl.ds(rows, 128), :] = value.astype(bf16)
-            gt[:, pl.ds(rows, 128)] = value.T.astype(bf16)
+            gt[0, :, pl.ds(rows, 128)] = value.T.astype(bf16)
             return carry
 
         lax.fori_loop(0, VW // 128, step, 0)
 
     turns = (wrap(x + 2), wrap(x + 1), wrap(x - 1), x)
 
-    def products_other(k):
+    def products(k):
         i = turns[k]
-        rows = jnp.dot(gt[...], w[i * 2 + 1 - c], preferred_element_type=f32)
-        wr[i] = rows.astype(bf16).reshape(4, 4, R, WIDTH)
-        send(wr.at[i], g.at[c, i, :, :, :, pl.ds(WIDTH, WIDTH)], y_send, y_recv.at[k], device(dc=1))
-
-    def products_own(k):
-        i = turns[k]
-        rows = jnp.dot(gt[...], w[i * 2 + c], preferred_element_type=f32)
-        wait(g.at[1 - c, i, :, :, :, pl.ds(WIDTH, WIDTH)], y_recv.at[k])
-        rows += g[1 - c, i, :, :, :, WIDTH:2 * WIDTH].reshape(T, WIDTH).astype(f32)
+        both = jnp.concatenate([gt[0], gt[1]], axis=1)
+        rows = jnp.dot(both, jnp.concatenate([w[i * 2 + c], w2[i]], axis=0), preferred_element_type=f32)
         wr[4 + i] = rows.astype(bf16).reshape(4, 4, R, WIDTH)
+
+    def grads_swap():
+        send(gt.at[0], gt.at[1], swap_send.at[1], swap_recv.at[1], device(dc=1))
+
+    def grads_swap_wait():
+        wait(w2, swap_recv.at[0])
+        wait(gt.at[1], swap_recv.at[1])
 
     def order(r):
         a1, a2, a3 = SUM_ORDERS[r]
@@ -456,7 +459,8 @@
         for phase in range(2):
             n = len(groups[phase])
             wait(st_r.at[pl.ds(starts[phase], n)], st_send.at[phase])
-        wait(wr.at[pl.ds(0, 4)], y_send)
+        wait(w2, swap_send.at[0])
+        wait(gt.at[0], swap_send.at[1])
         wait(wr.at[pl.ds(0, 3)], rs_send.at[0])
         wait(wr.at[0, pl.ds(0, 3)], rs_send.at[1])
         wait(t2.at[pl.ds(0, 3)], rs_send.at[2])
@@ -483,8 +487,8 @@
     early_core_wait(1)
     early_logits(1 - c, 1, 2, 2)
     ag8(0)
+    late_logits(0, c)
     ag8(1)
-    late_logits(0, c)
     late_logits(1, c)
     early_logits(c, 2, 1)
     early_core_wait(2)
@@ -498,47 +502,44 @@
     stats_send(1)
     stats_wait(1)
     grads()
-    products_other(0)
-    products_other(1)
-    products_own(0)
+    grads_swap()
+    head(0, 2)
+    grads_swap_wait()
+    products(0)
     rs3_start(0)
-    products_other(2)
-    products_own(1)
+    products(1)
     rs3_start(1)
+    products(2)
+    rs3_start(2)
     rs3_raw(0)
-    products_other(3)
-    products_own(2)
-    rs3_start(2)
     rs3_middle(0)
     rs3_raw(1)
-    products_own(3)
+    products(3)
     rs3_start(3)
     rs3_middle(1)
     rs3_raw(2)
     rs3_middle_x()
+    rs3_middle(2)
     rs3_raw(3)
-    rs3_middle(2)
-    head(0, 1)
+    head(2, 3)
     rs3_middle(3)
-    head(1, 2)
     rs3_end_lines(0)
-    head(2, 3)
+    head(3, 4)
+    rs3_end(1)
     rs3_end_lines(1)
-    rs3_end(1)
-    head(3, 4)
     rs3_end_lines(2)
     rs2_middle(0)
     rs2_middle(2)
     rs2_middle(1)
     head(4, 6)
     rs3_end_lines(3)
-    rs2_end(1)
     rs2_end(0)
     rs2_end(2)
+    rs2_end(1)
     head(6, 8)
-    rs1_end(1)
     rs1_end(0)
     rs1_end(2)
+    rs1_end(1)
     drain()
 
 
@@ -558,10 +559,11 @@
             pltpu.VMEM((2, 4, 4, 4, R, 2 * WIDTH), bf16),
             pltpu.VMEM((8, VW, WIDTH), bf16),
             pltpu.VMEM((8, 4, 4, R, WIDTH), bf16),
+            pltpu.VMEM((4, VW, WIDTH), bf16),
             pltpu.VMEM((VW, T), f32),
             pltpu.VMEM((VW, T), f32),
             pltpu.VMEM((VW, T), bf16),
-            pltpu.VMEM((T, VW), bf16),
+            pltpu.VMEM((2, T, VW), bf16),
             pltpu.VMEM((3, 8, T // 2), f32),
             pltpu.VMEM((22, 8, T // 2), f32),
             pltpu.VMEM((4, 4, R, WIDTH), bf16),
@@ -580,15 +582,15 @@
             dma((ROUNDS, PARTS, 3)),
             dma((2,)),
             dma((2,)),
-            dma,
-            dma((4,)),
+            dma((2,)),
+            dma((2,)),
             dma((3,)),
             dma((3, 3, 4)),
             dma((3, 3)),
             dma((3,)),
         ],
         compiler_params=pltpu.CompilerParams(
-            collective_id=0, has_side_effects=True, vmem_limit_bytes=46 * 2**20
+            collective_id=0, has_side_effects=True, vmem_limit_bytes=50 * 2**20
         ),
         cost_estimate=pl.CostEstimate(flops=4 * 2 * 512 * 512 * 8192, bytes_accessed=3 * 2**23, transcendentals=2**20),
         name="head_step",

time: 94.8 us -> 93 us (0.981)
  Pallas kernels: 90 us -> 88.1 us
    pallas_call x1, Pallas kernels: 90 us -> 88.1 us  [shards(): pl.pallas_call(kernel, out_shape=(pltpu.VMEM((R, WIDTH), f32), pltpu.VMEM...]
where the time goes in v4:
time: 93 us; the launch traced here: 92.8 us
  Pallas kernels  88.1 us (95%)
  local copies, waits for them, and re-layouts  4.05 us (4%)
    pallas_call x1, Pallas kernels, shards(): pl.pallas_call(kernel, out_shape=(pltpu.VMEM((R, WIDTH), f32), pltpu.VMEM...  88.1 us
    unnamed x2, local copies, waits for them, and re-layouts  4.05 us

profile of v4, /device:TPU:0, one launch (start us, length us, event | category | flops | bytes accessed | tf_op | source)
XLA Modules:
  0.0 92.8 jit_solution(9069608079185881788)
XLA Ops:
  0.6 88.1 %head_step.1 = (f32[32,1024]{1,0:T(8,128)S(1)}, bf16[512,8192]{1,0:T(8,128)(2,1)S(1)}) custom-call(bf16[32,1024]{1,0:T(8,128)(2,1)} %hid.1, bf16[32,1024]{1,0:T(8,128)(2,1)} %rhid.1, bf16[512,8192]{1,0:T(8,128)(2,1)} %w_hbm.1, bf16[4,4,32,8192]{3,2,1,0:T(8,128)(2,1)} %bitcast.4, s32[1,512]{1,0:T(1,128)} %bitcast.5, s32[1,512]{1,0:T(1,128)} %bitcast.6, ...), custom_call_target="tpu_custom_call" | custom-call | flops 17179869184 | bytes 25165824 | tf_op jit(solution)/shard_map/head_step/pallas_call | solution.py:550
  88.7 0.7 copy.11
  89.4 3.4 %copy.12 = bf16[512,8192]{1,0:T(8,128)(2,1)} copy(bf16[512,8192]{1,0:T(8,128)(2,1)S(1)} %get-tuple-element.3) | data formatting | bytes 16777216

commit v5 on v4

--- a/solution.py
+++ b/solution.py
@@ -299,6 +299,8 @@
             value = weight * (adv * (p - target) + penalty_weight * p * (lp - rlp - divergence))
             gv[pl.ds(rows, 128), :] = value.astype(bf16)
             gt[0, :, pl.ds(rows, 128)] = value.T.astype(bf16)
+            part = pl.ds(rows, 128)
+            send(gt.at[0, :, part], gt.at[1, :, part], swap_send.at[1], swap_recv.at[1], device(dc=1))
             return carry
 
         lax.fori_loop(0, VW // 128, step, 0)
@@ -310,9 +312,6 @@
         both = jnp.concatenate([gt[0], gt[1]], axis=1)
         rows = jnp.dot(both, jnp.concatenate([w[i * 2 + c], w2[i]], axis=0), preferred_element_type=f32)
         wr[4 + i] = rows.astype(bf16).reshape(4, 4, R, WIDTH)
-
-    def grads_swap():
-        send(gt.at[0], gt.at[1], swap_send.at[1], swap_recv.at[1], device(dc=1))
 
     def grads_swap_wait():
         wait(w2, swap_recv.at[0])
@@ -502,8 +501,7 @@
     stats_send(1)
     stats_wait(1)
     grads()
-    grads_swap()
-    head(0, 2)
+    head(0, 1)
     grads_swap_wait()
     products(0)
     rs3_start(0)
@@ -521,7 +519,7 @@
     rs3_middle_x()
     rs3_middle(2)
     rs3_raw(3)
-    head(2, 3)
+    head(1, 3)
     rs3_middle(3)
     rs3_end_lines(0)
     head(3, 4)

time: 93 us -> 92.8 us (level)
  no operation moved by 1% of the time
where the time goes in v5:
time: 92.8 us; the launch traced here: 92.6 us
  Pallas kernels  88 us (95%)
  local copies, waits for them, and re-layouts  4.05 us (4%)
    pallas_call x1, Pallas kernels, shards(): pl.pallas_call(kernel, out_shape=(pltpu.VMEM((R, WIDTH), f32), pltpu.VMEM...  88 us
    unnamed x2, local copies, waits for them, and re-layouts  4.05 us

profile of v5, /device:TPU:0, one launch (start us, length us, event | category | flops | bytes accessed | tf_op | source)
XLA Modules:
  0.0 92.6 jit_solution(8358161588118389462)
XLA Ops:
  0.6 88.0 %head_step.1 = (f32[32,1024]{1,0:T(8,128)S(1)}, bf16[512,8192]{1,0:T(8,128)(2,1)S(1)}) custom-call(bf16[32,1024]{1,0:T(8,128)(2,1)} %hid.1, bf16[32,1024]{1,0:T(8,128)(2,1)} %rhid.1, bf16[512,8192]{1,0:T(8,128)(2,1)} %w_hbm.1, bf16[4,4,32,8192]{3,2,1,0:T(8,128)(2,1)} %bitcast.4, s32[1,512]{1,0:T(1,128)} %bitcast.5, s32[1,512]{1,0:T(1,128)} %bitcast.6, ...), custom_call_target="tpu_custom_call" | custom-call | flops 17179869184 | bytes 25165824 | tf_op jit(solution)/shard_map/head_step/pallas_call | solution.py:548
  88.6 0.7 copy.11
  89.2 3.4 %copy.12 = bf16[512,8192]{1,0:T(8,128)(2,1)} copy(bf16[512,8192]{1,0:T(8,128)(2,1)S(1)} %get-tuple-element.3) | data formatting | bytes 16777216
